TPU v7x, 256 devices: a whole 4x4x8 slice. The times are simulated.
256 devices in a mesh: tile: 32 (over x, z_hi, core), tracer: 8 (over y, z_lo).
Axes of the slice: x: 4, y: 4, z: 8 (z_hi: 4, z_lo: 2; z = z_hi * 2 + z_lo), core: 2. Of those that a mesh axis runs over, the one named last changes fastest.
Arguments:
- tracers: float32 [16, 32, 8, 128, 128], P('tracer', 'tile'), may hold values from -16 to 16
- east_velocity: bfloat16 [32, 8, 128, 128], P('tile', 'tracer'), may hold values from -0.5 to 0.5
- north_velocity: bfloat16 [32, 8, 128, 128], P('tile', 'tracer'), may hold values from -0.5 to 0.5
- diffusivity: bfloat16 [32, 8], P('tile', 'tracer'), may hold values from 0.0099487305 to 0.14941406
- vertical_diffusivity: float32 [8], replicated, may hold values from 0.02 to 0.2
- depths: int32 [32], replicated, may hold values from 1 to 8
- neighbours: int32 [32, 4], replicated, may hold values from -1 to 31, as said below
Outputs:
- transported: float32 [16, 32, 8, 128, 128], P('tracer', 'tile')
Inputs may be any that keep to these rules, and one draw needn't show every extreme that they name: `neighbours`: tiles are the wet places of a face of 2 x 24 tile places, numbered row by row. Entry [s, e] is the slot of the wet tile beside slot s to the west, east, south or north (e = 0, 1, 2, 3), or -1 where that place is land or off the strip. The relation is symmetric; a west or east neighbour of slot s is s - 1 or s + 1, and a south or north neighbour lies at most 2 slots below or above s. The first 10 rows of places and the last 3 places hold no land.
All inputs are finite; a program needn't handle non-finite values.
Results may differ from a plain program's by a relative error of at most 0.0003.
Values may be sent and summed in bfloat16 or wider, within the bound.
No kernel may reach another device: no remote copies, remote signals or barrier semaphores. Data moves between devices by JAX's collectives and lax.ppermute only.
A program may use at most 64 MiB of HBM per device.

v0:
```python
import jax
import jax.numpy as jnp
from jax import lax
from jax.experimental import pallas as pl
from jax.experimental.pallas import tpu as pltpu
from jax.sharding import PartitionSpec as P

S = 128
LEVELS = 8
TILES = 32
AHEAD = (-2.0, 15.0, -60.0, 20.0, 30.0, -3.0, 0.0)
BEHIND = (0.0, 3.0, -30.0, -20.0, 60.0, -15.0, 2.0)
CURVE = (0.0, 0.0, 1.0, -2.0, 1.0, 0.0, 0.0)
BANDS = (AHEAD, BEHIND, CURVE)

MATES = [(s, s ^ 1) for s in range(TILES)]
ACROSS = [(s, s + 3) for s in range(0, TILES - 3, 2)] + [(s + 3, s) for s in range(0, TILES - 3, 2)]


def beside(neighbours, tile):
    row = [neighbours[tile, e] for e in range(4)]
    return [jnp.where(slot < 0, -9, slot) for slot in row]


def band(distance, coefficients):
    total = jnp.zeros(distance.shape, jnp.float32)
    for step, coefficient in zip(range(-3, 4), coefficients):
        if coefficient:
            total = jnp.where(distance == step, coefficient, total)
    return total


def iota(shape, dim):
    return lax.broadcasted_iota(jnp.int32, shape, dim)


def bands_right(source, width):
    out = iota((width, S), 1)
    return jnp.concatenate([band(source - out, c) for c in BANDS], 1).astype(jnp.bfloat16)


def bands_left(source, width):
    out = iota((S, width), 0)
    return jnp.concatenate([band(source - out, c) for c in BANDS], 0).astype(jnp.bfloat16)


def rims(read, side_east, tile, out):
    planes = 2 * LEVELS
    lane = iota((S, S), 1)
    shift = jnp.where(side_east, 4, 0)
    x_rim = jnp.zeros((S, S), jnp.float32)
    for p in range(planes):
        x_rim = jnp.where(lane // 4 == p, pltpu.roll(read(p), shift + 4 * p, 1), x_rim)
    half = S // 2
    x_rim = jnp.where(lane[:half] < half, x_rim[:half], pltpu.roll(x_rim[half:], half, 1))
    low = iota((8, S), 0) < 4
    south, north = [], []
    for p in range(0, planes, 2):
        first, second = read(p), read(p + 1)
        south.append(jnp.where(low, first[:8], pltpu.roll(second[:8], 4, 0)))
        north.append(jnp.where(low, pltpu.roll(first[S - 8 :], 4, 0), second[S - 8 :]))
    south, north = jnp.concatenate(south, 0), jnp.concatenate(north, 0)
    even = tile % 2 == 0
    out[0] = x_rim.astype(jnp.bfloat16)
    out[1] = jnp.where(even, south, north).astype(jnp.bfloat16)
    out[2] = jnp.where(even, north, south).astype(jnp.bfloat16)


def first_kernel(
    tracers_in,
    east_in,
    north_in,
    mixing_in,
    depths_in,
    neighbours_in,
    flow_out,
    rims_out,
    tracers,
    east,
    north,
    mixing,
    depths,
    neighbours,
    arrived,
):
    copies = [
        pltpu.make_async_copy(source, target, arrived.at[i])
        for i, (source, target) in enumerate(
            (
                (east_in, east),
                (north_in, north),
                (mixing_in, mixing),
                (depths_in, depths),
                (neighbours_in, neighbours),
                (tracers_in, tracers),
            )
        )
    ]
    for copy in copies:
        copy.start()
    for copy in copies[:3]:
        copy.wait()
    block = jnp.concatenate(
        [
            east[...],
            north[...],
            jnp.broadcast_to(mixing[...].astype(jnp.float32), (16, S)).astype(jnp.bfloat16),
        ],
        0,
    )
    for j in range(LEVELS):
        flow_out[j] = block
    for copy in copies[3:]:
        copy.wait()
    tile = lax.axis_index("tile")
    depth = depths[tile]

    def read(p):
        return tracers[p] * (p % LEVELS < depth).astype(jnp.float32)

    rims(read, neighbours[tile, 1] >= 0, tile, rims_out)


def substep(values, flow, near, tile, received, vertical, depth, emit):
    planes = 2 * LEVELS
    gx = jnp.zeros((S // 2, S), jnp.float32)
    gs = jnp.zeros((S // 2, S), jnp.float32)
    gn = jnp.zeros((S // 2, S), jnp.float32)
    mate, own, other = received
    toward = jnp.where(tile % 2 == 0, 1, -1)
    for steps, x_block, y_block in (
        (1, mate.at[0], mate.at[2]),
        (2, None, own.at[1]),
        (-1, other.at[0], other.at[1]),
        (-2, None, other.at[2]),
    ):
        slot = tile + steps * toward
        if x_block is not None:
            in_row = (slot == near[0]) | (slot == near[1])
            gx = jnp.where(in_row, x_block[...].astype(jnp.float32), gx)
        block = y_block[...].astype(jnp.float32)
        gs = jnp.where(slot == near[2], block, gs)
        gn = jnp.where(slot == near[3], block, gn)
    gx = jnp.concatenate([gx, pltpu.roll(gx, S // 2, 1)], 0)
    base = jnp.where(near[1] >= 0, S, -4)
    own_right = bands_right(iota((S, S), 0), S)
    right = jnp.concatenate([own_right, own_right], 0)
    ghost_right = bands_right(iota((S, S), 0) % 4 + base, S)
    own_left = bands_left(iota((S, S), 1), S)
    left = jnp.concatenate([own_left, own_left], 1)
    column = iota((S, 16), 1)
    source = jnp.where(column < 8, column % 4 - 4, column % 4 + S)
    ghost_left = [
        bands_left(jnp.where((column // 4) % 2 == odd, source, -2 * S), 16) for odd in range(2)
    ]
    lane_block = iota((S, S), 1) // 4

    def dot(a, b):
        return jnp.dot(a, b, preferred_element_type=jnp.float32)

    for k in range(LEVELS):
        pair = [values(k), values(k + LEVELS)]
        high = [q.astype(jnp.bfloat16) for q in pair]
        low = [(q - h.astype(jnp.float32)).astype(jnp.bfloat16) for q, h in zip(pair, high)]
        rows = jnp.concatenate(
            [jnp.concatenate([h, l], 1) for h, l in zip(high, low)], 0
        )
        ghosts = jnp.concatenate(
            [jnp.where(lane_block == p, gx, 0.0).astype(jnp.bfloat16) for p in (k, k + LEVELS)], 0
        )
        along_x = dot(rows, right) + dot(ghosts, ghost_right)
        columns = jnp.concatenate(
            [jnp.concatenate([h, l], 0) for h, l in zip(high, low)], 1
        )
        edge = jnp.concatenate(
            [
                jnp.concatenate([gs[8 * t : 8 * t + 8], gn[8 * t : 8 * t + 8]], 0)
                for t in (k // 2, (k + LEVELS) // 2)
            ],
            1,
        ).astype(jnp.bfloat16)
        along_y = dot(left, columns) + dot(ghost_left[k % 2], edge)
        u = flow[k, :S].astype(jnp.float32)
        v = flow[k, S : 2 * S].astype(jnp.float32)
        mixing = flow[k, 2 * S : 2 * S + 16].astype(jnp.float32)[:1]
        wet = (k < depth).astype(jnp.float32)
        lift = vertical[k]
        for t in range(2):
            x = along_x[t * S : (t + 1) * S]
            y = along_y[:, t * S : (t + 1) * S]
            q = pair[t]
            slope_x = jnp.where(u >= 0, x[:, :S], x[:, S : 2 * S])
            slope_y = jnp.where(v >= 0, y[:S], y[S : 2 * S])
            carry = (u * slope_x + v * slope_y) * (1.0 / 60.0)
            curve = x[:, 2 * S :] + y[2 * S :]
            column_sum = -2.0 * q
            if k > 0:
                column_sum = column_sum + values(k - 1 + t * LEVELS)
            if k < LEVELS - 1:
                column_sum = column_sum + values(k + 1 + t * LEVELS)
            emit(k + t * LEVELS, wet * (mixing * curve - carry + lift * column_sum))


def second_kernel(
    tracers, flow, vertical, depths, neighbours, mate, own, other, section, rims_out
):
    tile = lax.axis_index("tile")
    near = beside(neighbours, tile)
    depth = depths[tile]

    def start(p):
        return tracers[p] * (p % LEVELS < depth).astype(jnp.float32)

    def emit(p, change):
        section[p] = start(p) + change

    substep(start, flow, near, tile, (mate, own, other), vertical, depth, emit)
    rims(lambda p: section[p], near[1] >= 0, tile, rims_out)


def third_kernel(
    tracers, section, flow, vertical, depths, neighbours, mate, own, other, out
):
    tile = lax.axis_index("tile")
    near = beside(neighbours, tile)
    depth = depths[tile]

    def emit(p, change):
        start = tracers[p] * (p % LEVELS < depth).astype(jnp.float32)
        out[p] = 0.5 * (start + section[p] + change)

    received = (mate, own, other)
    substep(lambda p: section[p], flow, near, tile, received, vertical, depth, emit)


VMEM = pl.BlockSpec(memory_space=pltpu.VMEM)
SMEM = pl.BlockSpec(memory_space=pltpu.SMEM)
HBM = pl.BlockSpec(memory_space=pltpu.HBM)
PARAMS = pltpu.CompilerParams(vmem_limit_bytes=48 * 1024 * 1024)
RIMS = jax.ShapeDtypeStruct((3, S // 2, S), jnp.bfloat16)


def exchange(blocks):
    mate = lax.ppermute(blocks, "tile", MATES)
    own = lax.ppermute(jnp.concatenate([mate[:2], blocks[2:]], 0), "tile", ACROSS)
    return mate, own, lax.ppermute(own, "tile", MATES)


def local(
    tracers, east_velocity, north_velocity, diffusivity, vertical_diffusivity, depths, neighbours
):
    planes = 2 * LEVELS
    field = tracers.reshape(planes, S, S)
    flow, blocks = pl.pallas_call(
        first_kernel,
        out_shape=[jax.ShapeDtypeStruct((LEVELS, 2 * S + 16, S), jnp.bfloat16), RIMS],
        in_specs=[HBM] * 6,
        out_specs=[VMEM] * 2,
        scratch_shapes=[
            pltpu.VMEM((planes, S, S), jnp.float32),
            pltpu.VMEM((S, S), jnp.bfloat16),
            pltpu.VMEM((S, S), jnp.bfloat16),
            pltpu.VMEM((1, 1), jnp.bfloat16),
            pltpu.SMEM((TILES,), jnp.int32),
            pltpu.SMEM((TILES, 4), jnp.int32),
            pltpu.SemaphoreType.DMA((6,)),
        ],
        compiler_params=pltpu.CompilerParams(vmem_limit_bytes=62 * 1024 * 1024),
        name="rims",
    )(
        field,
        east_velocity.reshape(S, S),
        north_velocity.reshape(S, S),
        diffusivity,
        depths,
        neighbours,
    )
    flow = lax.all_to_all(flow, "tracer", 0, 0)
    section, blocks = pl.pallas_call(
        second_kernel,
        out_shape=[jax.ShapeDtypeStruct((planes, S, S), jnp.float32), RIMS],
        in_specs=[VMEM] * 2 + [SMEM] * 3 + [VMEM] * 3,
        out_specs=[VMEM] * 2,
        compiler_params=PARAMS,
        name="section",
    )(field, flow, vertical_diffusivity, depths, neighbours, *exchange(blocks))
    out = pl.pallas_call(
        third_kernel,
        out_shape=jax.ShapeDtypeStruct((planes, S, S), jnp.float32),
        in_specs=[VMEM] * 3 + [SMEM] * 3 + [VMEM] * 3,
        out_specs=VMEM,
        compiler_params=PARAMS,
        name="transported",
    )(field, section, flow, vertical_diffusivity, depths, neighbours, *exchange(blocks))
    return out.reshape(tracers.shape)


def solution(mesh):
    return jax.shard_map(
        local,
        mesh=mesh,
        in_specs=(
            P("tracer", "tile", None, None, None),
            P("tile", "tracer", None, None),
            P("tile", "tracer", None, None),
            P("tile", "tracer"),
            P(),
            P(),
            P(),
        ),
        out_specs=P("tracer", "tile", None, None, None),
        check_vma=False,
    )
```

profile of v0, /device:TPU:15, one launch (start us, length us, event | category | flops | bytes accessed | tf_op | source)
XLA Modules:
  0.0 42.8 jit_solution(10408704435378642080)
XLA Ops:
  0.7 1.4 %copy.8.neighbours_in.neighbours = s32[32,4]{1,0:T(8,128)} copy(s32[32,4]{0,1:T(4,128)} %param.13) | data formatting | bytes 1024 | tf_op args[6]
  2.0 0.0 copy-start
  2.0 2.3 %rims.1 = (bf16[8,272,128]{2,1,0:T(8,128)(2,1)}, bf16[3,64,128]{2,1,0:T(8,128)(2,1)}) custom-call(f32[16,128,128]{2,1,0:T(8,128)} %bitcast.6, bf16[128,128]{1,0:T(8,128)(2,1)} %bitcast.9, bf16[128,128]{1,0:T(8,128)(2,1)} %bitcast.10, bf16[1,1]{1,0:T(2,128)(2,1)S(6)} %copy.12.mixing_in, s32[32]{0:T(128)} %depths.3, s32[32,4]{1,0:T(8,128)} %copy.8.neighbours_in.neighbours), custom_call_target="tpu_custom_call" | custom-call | tf_op jit(solution)/shard_map/rims/pallas_call | solution.py:254
  4.3 0.0 copy-start.4
  4.3 5.9 %all-to-all-start = ((bf16[8,272,128]{2,1,0:T(8,128)(2,1)}), bf16[8,272,128]{2,1,0:T(8,128)(2,1)S(1)}, u32[]{:S(2)}, u32[]{:S(2)}) async-start(bf16[8,272,128]{2,1,0:T(8,128)(2,1)} %get-tuple-element.9), calls=%async_computation | async-start | bytes 1114112 | tf_op jit(solution)/shard_map/all_to_all | solution.py:278
  10.2 0.0 copy-done.4
  10.2 1.2 %collective-permute-start = (bf16[3,64,128]{2,1,0:T(8,128)(2,1)S(1)}, bf16[3,64,128]{2,1,0:T(8,128)(2,1)S(1)}, u32[]{:S(2)}, u32[]{:S(2)}) collective-permute-start(bf16[3,64,128]{2,1,0:T(8,128)(2,1)S(1)} %copy-done.4), channel_id=1, source_target_pairs={{0,8},{8,0},{16,24},{24,16},{32,40},{40,32},{48,56},{56,48},{64,72... | collective-permute-start | bytes 147464 | tf_op jit(solution)/shard_map/ppermute | solution.py:244
  11.4 0.9 %collective-permute-done.mate = bf16[3,64,128]{2,1,0:T(8,128)(2,1)S(1)} collective-permute-done((bf16[3,64,128]{2,1,0:T(8,128)(2,1)S(1)}, bf16[3,64,128]{2,1,0:T(8,128)(2,1)S(1)}, u32[]{:S(2)}, u32[]{:S(2)}) %collective-permute-start) | collective-permute-done | bytes 49184 | tf_op jit(solution)/shard_map/ppermute | solution.py:244
  12.3 0.0 copy-start.1
  12.3 0.0 copy-start.2
  12.3 0.0 copy-start.3
  12.3 7.7 %collective-permute-start.1 = (bf16[3,64,128]{2,1,0:T(8,128)(2,1)S(1)}, bf16[3,64,128]{2,1,0:T(8,128)(2,1)S(1)}, u32[]{:S(2)}, u32[]{:S(2)}) collective-permute-start(bf16[3,64,128]{2,1,0:T(8,128)(2,1)S(1)} %pad_maximum_fusion), channel_id=1, source_target_pairs={{0,24},{16,40},{32,56},{48,72},{64,88},{80,104},{96,120},{112,136}... | collective-permute-start | bytes 147464 | tf_op jit(solution)/shard_map/ppermute | solution.py:245
  20.0 3.3 %collective-permute-done.1.own = bf16[3,64,128]{2,1,0:T(8,128)(2,1)S(1)} collective-permute-done((bf16[3,64,128]{2,1,0:T(8,128)(2,1)S(1)}, bf16[3,64,128]{2,1,0:T(8,128)(2,1)S(1)}, u32[]{:S(2)}, u32[]{:S(2)}) %collective-permute-start.1) | collective-permute-done | bytes 49184 | tf_op jit(solution)/shard_map/ppermute | solution.py:245
  23.3 0.0 collective-permute-start.2
  23.3 1.2 %collective-permute-done.2.other = bf16[3,64,128]{2,1,0:T(8,128)(2,1)S(1)} collective-permute-done((bf16[3,64,128]{2,1,0:T(8,128)(2,1)S(1)}, bf16[3,64,128]{2,1,0:T(8,128)(2,1)S(1)}, u32[]{:S(2)}, u32[]{:S(2)}) %collective-permute-start.2) | collective-permute-done | bytes 49184 | tf_op jit(solution)/shard_map/ppermute | solution.py:246
  24.5 0.0 all-to-all-done.flow
  24.5 0.0 copy-done
  24.5 0.0 copy-done.1
  24.5 0.0 copy-done.2
  24.5 0.0 copy-done.3
  24.5 3.2 %section.1 = (f32[16,128,128]{2,1,0:T(8,128)S(1)}, bf16[3,64,128]{2,1,0:T(8,128)(2,1)S(1)}) custom-call(f32[16,128,128]{2,1,0:T(8,128)S(1)} %bitcast.7, bf16[8,272,128]{2,1,0:T(8,128)(2,1)S(1)} %all-to-all-done.flow, f32[8]{0:T(128)S(1)} %copy-done.3, s32[32]{0:T(128)S(1)} %copy-done.2, s32[32,4]{1,0:T(8,128)S(1)} %copy-done.1, ...), custom_call_target="tpu_custom_call" | custom-call | tf_op jit(solution)/shard_map/section/pallas_call | solution.py:279
  27.7 0.2 collective-permute-start.3
  28.0 1.1 %collective-permute-done.3.mate = bf16[3,64,128]{2,1,0:T(8,128)(2,1)S(1)} collective-permute-done((bf16[3,64,128]{2,1,0:T(8,128)(2,1)S(1)}, bf16[3,64,128]{2,1,0:T(8,128)(2,1)S(1)}, u32[]{:S(2)}, u32[]{:S(2)}) %collective-permute-start.3) | collective-permute-done | bytes 49184 | tf_op jit(solution)/shard_map/ppermute | solution.py:244
  29.1 5.2 %collective-permute-start.4 = (bf16[3,64,128]{2,1,0:T(8,128)(2,1)S(1)}, bf16[3,64,128]{2,1,0:T(8,128)(2,1)S(1)}, u32[]{:S(2)}, u32[]{:S(2)}) collective-permute-start(bf16[3,64,128]{2,1,0:T(8,128)(2,1)S(1)} %pad_maximum_fusion.1), channel_id=1, source_target_pairs={{0,24},{16,40},{32,56},{48,72},{64,88},{80,104},{96,120},{112,136}... | collective-permute-start | bytes 147464 | tf_op jit(solution)/shard_map/ppermute | solution.py:245
  34.2 3.3 %collective-permute-done.4.own = bf16[3,64,128]{2,1,0:T(8,128)(2,1)S(1)} collective-permute-done((bf16[3,64,128]{2,1,0:T(8,128)(2,1)S(1)}, bf16[3,64,128]{2,1,0:T(8,128)(2,1)S(1)}, u32[]{:S(2)}, u32[]{:S(2)}) %collective-permute-start.4) | collective-permute-done | bytes 49184 | tf_op jit(solution)/shard_map/ppermute | solution.py:245
  37.5 0.0 collective-permute-start.5
  37.5 1.2 %collective-permute-done.5.other = bf16[3,64,128]{2,1,0:T(8,128)(2,1)S(1)} collective-permute-done((bf16[3,64,128]{2,1,0:T(8,128)(2,1)S(1)}, bf16[3,64,128]{2,1,0:T(8,128)(2,1)S(1)}, u32[]{:S(2)}, u32[]{:S(2)}) %collective-permute-start.5) | collective-permute-done | bytes 49184 | tf_op jit(solution)/shard_map/ppermute | solution.py:246
  38.7 4.1 %transported.1 = f32[16,128,128]{2,1,0:T(8,128)} custom-call(f32[16,128,128]{2,1,0:T(8,128)S(1)} %bitcast.8, f32[16,128,128]{2,1,0:T(8,128)S(1)} %get-tuple-element.11.section, bf16[8,272,128]{2,1,0:T(8,128)(2,1)S(1)} %all-to-all-done.flow, f32[8]{0:T(128)S(1)} %copy-done.3, s32[32]{0:T(128)S(1)} %copy-done.2, s32[32,4]{1,0:T(8,128)S(1)} %copy-done.1, ...), custom_call_target="tpu_custom_call" | custom-call | tf_op jit(solution)/shard_map/transported/pallas_call | solution.py:287
  (6 shorter events, 0.0 us)
Async XLA Ops:
  2.0 22.5 %copy-start = (f32[2,1,8,128,128]{4,3,2,1,0:T(8,128)S(1)}, f32[2,1,8,128,128]{4,3,2,1,0:T(8,128)}, u32[]{:S(2)}) copy-start(f32[2,1,8,128,128]{4,3,2,1,0:T(8,128)} %param.7) | copy-start | bytes 3145732
  4.3 5.9 %copy-start.4 = (bf16[3,64,128]{2,1,0:T(8,128)(2,1)S(1)}, bf16[3,64,128]{2,1,0:T(8,128)(2,1)}, u32[]{:S(2)}) copy-start(bf16[3,64,128]{2,1,0:T(8,128)(2,1)} %get-tuple-element.10) | copy-start | bytes 147460
  4.3 20.2 %all-to-all-start = ((bf16[8,272,128]{2,1,0:T(8,128)(2,1)}), bf16[8,272,128]{2,1,0:T(8,128)(2,1)S(1)}, u32[]{:S(2)}, u32[]{:S(2)}) async-start(bf16[8,272,128]{2,1,0:T(8,128)(2,1)} %get-tuple-element.9), calls=%async_computation | async-start | bytes 1114112 | tf_op jit(solution)/shard_map/all_to_all | solution.py:278
  10.2 2.1 %collective-permute-start = (bf16[3,64,128]{2,1,0:T(8,128)(2,1)S(1)}, bf16[3,64,128]{2,1,0:T(8,128)(2,1)S(1)}, u32[]{:S(2)}, u32[]{:S(2)}) collective-permute-start(bf16[3,64,128]{2,1,0:T(8,128)(2,1)S(1)} %copy-done.4), channel_id=1, source_target_pairs={{0,8},{8,0},{16,24},{24,16},{32,40},{40,32},{48,56},{56,48},{64,72... | collective-permute-start | bytes 147464 | tf_op jit(solution)/shard_map/ppermute | solution.py:244
  12.3 12.2 %copy-start.1 = (s32[32,4]{1,0:T(8,128)S(1)}, s32[32,4]{1,0:T(8,128)}, u32[]{:S(2)}) copy-start(s32[32,4]{1,0:T(8,128)} %copy.8.neighbours_in.neighbours) | copy-start | bytes 1540
  12.3 12.2 %copy-start.2 = (s32[32]{0:T(128)S(1)}, s32[32]{0:T(128)}, u32[]{:S(2)}) copy-start(s32[32]{0:T(128)} %depths.3) | copy-start | bytes 388
  12.3 12.2 %copy-start.3 = (f32[8]{0:T(128)S(1)}, f32[8]{0:T(128)}, u32[]{:S(2)}) copy-start(f32[8]{0:T(128)} %vertical.3) | copy-start | bytes 100
  12.3 10.9 %collective-permute-start.1 = (bf16[3,64,128]{2,1,0:T(8,128)(2,1)S(1)}, bf16[3,64,128]{2,1,0:T(8,128)(2,1)S(1)}, u32[]{:S(2)}, u32[]{:S(2)}) collective-permute-start(bf16[3,64,128]{2,1,0:T(8,128)(2,1)S(1)} %pad_maximum_fusion), channel_id=1, source_target_pairs={{0,24},{16,40},{32,56},{48,72},{64,88},{80,104},{96,120},{112,136}... | collective-permute-start | bytes 147464 | tf_op jit(solution)/shard_map/ppermute | solution.py:245
  23.3 1.2 %collective-permute-start.2 = (bf16[3,64,128]{2,1,0:T(8,128)(2,1)S(1)}, bf16[3,64,128]{2,1,0:T(8,128)(2,1)S(1)}, u32[]{:S(2)}, u32[]{:S(2)}) collective-permute-start(bf16[3,64,128]{2,1,0:T(8,128)(2,1)S(1)} %collective-permute-done.1.own), channel_id=1, source_target_pairs={{0,8},{8,0},{16,24},{24,16},{32,40},{40,32},{48,56},{56,48},{64,72... | collective-permute-start | bytes 147464 | tf_op jit(solution)/shard_map/ppermute | solution.py:246
  27.7 1.3 %collective-permute-start.3 = (bf16[3,64,128]{2,1,0:T(8,128)(2,1)S(1)}, bf16[3,64,128]{2,1,0:T(8,128)(2,1)S(1)}, u32[]{:S(2)}, u32[]{:S(2)}) collective-permute-start(bf16[3,64,128]{2,1,0:T(8,128)(2,1)S(1)} %get-tuple-element.12), channel_id=1, source_target_pairs={{0,8},{8,0},{16,24},{24,16},{32,40},{40,32},{48,56},{56,48},{64,72... | collective-permute-start | bytes 147464 | tf_op jit(solution)/shard_map/ppermute | solution.py:244
  29.1 8.4 %collective-permute-start.4 = (bf16[3,64,128]{2,1,0:T(8,128)(2,1)S(1)}, bf16[3,64,128]{2,1,0:T(8,128)(2,1)S(1)}, u32[]{:S(2)}, u32[]{:S(2)}) collective-permute-start(bf16[3,64,128]{2,1,0:T(8,128)(2,1)S(1)} %pad_maximum_fusion.1), channel_id=1, source_target_pairs={{0,24},{16,40},{32,56},{48,72},{64,88},{80,104},{96,120},{112,136}... | collective-permute-start | bytes 147464 | tf_op jit(solution)/shard_map/ppermute | solution.py:245
  37.5 1.2 %collective-permute-start.5 = (bf16[3,64,128]{2,1,0:T(8,128)(2,1)S(1)}, bf16[3,64,128]{2,1,0:T(8,128)(2,1)S(1)}, u32[]{:S(2)}, u32[]{:S(2)}) collective-permute-start(bf16[3,64,128]{2,1,0:T(8,128)(2,1)S(1)} %collective-permute-done.4.own), channel_id=1, source_target_pairs={{0,8},{8,0},{16,24},{24,16},{32,40},{40,32},{48,56},{56,48},{64,72... | collective-permute-start | bytes 147464 | tf_op jit(solution)/shard_map/ppermute | solution.py:246
where the time goes:
time: 43.1 us; the launch traced here: 42.8 us
  starting transfers between devices  20.2 us (47%)
  waiting for transfers between devices  10.9 us (25%)
  Pallas kernels  9.57 us (22%)
  local copies, waits for them, and re-layouts  1.39 us (3%)
  between operations  0.74 us (2%)
    ppermute x2, starting transfers between devices, exchange(): lax.ppermute(jnp.concatenate([mate[:2], blocks[2:]], 0), 'tile', ACROSS)  12.8 us
    ppermute x2, waiting for transfers between devices, exchange(): lax.ppermute(jnp.concatenate([mate[:2], blocks[2:]], 0), 'tile', ACROSS)  6.5 us
    all_to_all x1, starting transfers between devices, local(): flow = lax.all_to_all(flow, 'tracer', 0, 0)  5.85 us
    pallas_call x1, Pallas kernels, local(): pl.pallas_call(third_kernel, out_shape=jax.ShapeDtypeStruct((planes, S, S...  4.07 us
    pallas_call x1, Pallas kernels, local(): pl.pallas_call(second_kernel, out_shape=[jax.ShapeDtypeStruct((planes, S,...  3.21 us
    ppermute x2, waiting for transfers between devices, exchange(): return (mate, own, lax.ppermute(own, 'tile', MATES))  2.46 us
    pallas_call x1, Pallas kernels, local(): pl.pallas_call(first_kernel, out_shape=[jax.ShapeDtypeStruct((LEVELS, 2 *...  2.28 us
    ppermute x2, waiting for transfers between devices, exchange(): mate = lax.ppermute(blocks, 'tile', MATES)  1.95 us
  transfers between devices with their start and end apart: 7, of which 6 were waited for; matrix products, arithmetic and copies ran while one was open for 0% of the time, Pallas kernels for 0%

commit v1 on v0

v1 whole, which is shorter than its diff:
```python
import jax
import jax.numpy as jnp
from jax import lax
from jax.experimental import pallas as pl
from jax.experimental.pallas import tpu as pltpu
from jax.sharding import PartitionSpec as P

S = 128
LEVELS = 8
TILES = 32
AHEAD = (-2.0, 15.0, -60.0, 20.0, 30.0, -3.0, 0.0)
BEHIND = (0.0, 3.0, -30.0, -20.0, 60.0, -15.0, 2.0)
CURVE = (0.0, 0.0, 1.0, -2.0, 1.0, 0.0, 0.0)
BANDS = (AHEAD, BEHIND, CURVE)

MATES = [(s, s ^ 1) for s in range(TILES)]
ACROSS = [(s, s + 3) for s in range(0, TILES - 3, 2)] + [(s + 3, s) for s in range(0, TILES - 3, 2)]


def beside(neighbours, tile):
    row = [neighbours[e, tile] for e in range(4)]
    return [jnp.where(slot < 0, -9, slot) for slot in row]


def band(distance, coefficients):
    total = jnp.zeros(distance.shape, jnp.float32)
    for step, coefficient in zip(range(-3, 4), coefficients):
        if coefficient:
            total = jnp.where(distance == step, coefficient, total)
    return total


def iota(shape, dim):
    return lax.broadcasted_iota(jnp.int32, shape, dim)


def bands_right(source, width):
    out = iota((width, S), 1)
    return jnp.concatenate([band(source - out, c) for c in BANDS], 1).astype(jnp.bfloat16)


def bands_left(source, out):
    return jnp.concatenate([band(source - out, c) for c in BANDS], 0).astype(jnp.bfloat16)


def rims(read, side_east, tile, out):
    planes = 2 * LEVELS
    lane = iota((S, S), 1)
    shift = jnp.where(side_east, 4, 0)
    x_rim = jnp.zeros((S, S), jnp.float32)
    for p in range(planes):
        x_rim = jnp.where(lane // 4 == p, pltpu.roll(read(p), shift + 4 * p, 1), x_rim)
    half = S // 2
    x_rim = jnp.where(lane[:half] < half, x_rim[:half], pltpu.roll(x_rim[half:], half, 1))
    low = iota((8, S), 0) < 4
    south, north = [], []
    for p in range(0, planes, 2):
        first, second = read(p), read(p + 1)
        south.append(jnp.where(low, first[:8], pltpu.roll(second[:8], 4, 0)))
        north.append(jnp.where(low, pltpu.roll(first[S - 8 :], 4, 0), second[S - 8 :]))
    south, north = jnp.concatenate(south, 0), jnp.concatenate(north, 0)
    even = tile % 2 == 0
    out[0] = x_rim.astype(jnp.bfloat16)
    out[1] = jnp.where(even, south, north).astype(jnp.bfloat16)
    out[2] = jnp.where(even, north, south).astype(jnp.bfloat16)


def first_kernel(
    tracers_in,
    east_in,
    north_in,
    mixing,
    depths_in,
    neighbours_in,
    vertical_in,
    flow_out,
    rims_out,
    start_out,
    levels_out,
    tracers,
    east,
    north,
    depths,
    neighbours,
    vertical,
    arrived,
):
    copies = [
        pltpu.make_async_copy(source, target, arrived.at[i])
        for i, (source, target) in enumerate(
            (
                (east_in, east),
                (north_in, north),
                (depths_in, depths),
                (neighbours_in, neighbours),
                (vertical_in, vertical),
                (tracers_in, tracers),
            )
        )
    ]
    for copy in copies:
        copy.start()
    for copy in copies[:2]:
        copy.wait()
    block = jnp.concatenate(
        [
            east[...],
            north[...],
            jnp.broadcast_to(mixing[...].astype(jnp.float32), (16, S)).astype(jnp.bfloat16),
        ],
        0,
    )
    for j in range(LEVELS):
        flow_out[j] = block
    for copy in copies[2:]:
        copy.wait()
    tile = lax.axis_index("tile")
    depth = depths[tile]

    for k in range(LEVELS):
        wet = (k < depth).astype(jnp.float32)
        levels_out[k : k + 1] = jnp.full((1, S), wet, jnp.float32)
        levels_out[LEVELS + k : LEVELS + k + 1] = jnp.full((1, S), wet * vertical[k], jnp.float32)
    for p in range(2 * LEVELS):
        start_out[p] = tracers[p] * (p % LEVELS < depth).astype(jnp.float32)
    rims(lambda p: start_out[p], neighbours[1, tile] >= 0, tile, rims_out)


def ghosts(near, tile, received):
    gx, gs, gn = (jnp.zeros((S // 2, S), jnp.float32) for _ in range(3))
    mate, own, other = received
    toward = jnp.where(tile % 2 == 0, 1, -1)
    for steps, x_block, y_block in (
        (1, mate.at[0], mate.at[2]),
        (2, None, own.at[1]),
        (-1, other.at[0], other.at[1]),
        (-2, None, other.at[2]),
    ):
        slot = tile + steps * toward
        if x_block is not None:
            in_row = (slot == near[0]) | (slot == near[1])
            gx = jnp.where(in_row, x_block[...].astype(jnp.float32), gx)
        block = y_block[...].astype(jnp.float32)
        gs = jnp.where(slot == near[2], block, gs)
        gn = jnp.where(slot == near[3], block, gn)
    return jnp.concatenate([gx, pltpu.roll(gx, S // 2, 1)], 0), gs, gn


def dot(a, b):
    return jnp.dot(a, b, preferred_element_type=jnp.float32)


def inner_sums(values, emit):
    own_right = bands_right(iota((S, S), 0), S)
    right = jnp.concatenate([own_right, own_right], 0)
    own_left = bands_left(iota((S, S), 1), iota((S, S), 0))
    left = jnp.concatenate([own_left, own_left], 1)
    for k in range(LEVELS):
        pair = [values(k), values(k + LEVELS)]
        high = [q.astype(jnp.bfloat16) for q in pair]
        low = [(q - h.astype(jnp.float32)).astype(jnp.bfloat16) for q, h in zip(pair, high)]
        rows = jnp.concatenate([jnp.concatenate([h, l], 1) for h, l in zip(high, low)], 0)
        columns = jnp.concatenate([jnp.concatenate([h, l], 0) for h, l in zip(high, low)], 1)
        along_x = dot(rows, right)
        along_y = dot(left, columns)
        for t in range(2):
            z = -2.0 * pair[t]
            if k > 0:
                z = z + values(k - 1 + t * LEVELS)
            if k < LEVELS - 1:
                z = z + values(k + 1 + t * LEVELS)
            emit(k + t * LEVELS, along_x[t * S : (t + 1) * S], along_y[:, t * S : (t + 1) * S], z)


def rim_sums(near, tile, received):
    gx, gs, gn = ghosts(near, tile, received)
    base = jnp.where(near[1] >= 0, S, -4)
    right = jnp.concatenate([bands_right(iota((8, S), 0) % 4 + base, 8)] * (S // 8), 0)
    row = iota((16, 16), 0)
    row = jnp.where(row < 8, row, row + S - 16)
    column = iota((16, 16), 1)
    source = jnp.where(column < 8, column % 4 - 4, column % 4 + S)
    left = [
        bands_left(jnp.where((column // 4) % 2 == odd, source, -2 * S), row) for odd in range(2)
    ]
    lane_block = iota((S, S), 1) // 4

    def level(k):
        planes = (k, k + LEVELS)
        x_rims = [jnp.where(lane_block == p, gx, 0.0).astype(jnp.bfloat16) for p in planes]
        y_rims = [
            jnp.concatenate([g[8 * (p // 2) : 8 * (p // 2) + 8] for g in (gs, gn)], 0)
            for p in planes
        ]
        along_x = dot(jnp.concatenate(x_rims, 0), right)
        along_y = dot(left[k % 2], jnp.concatenate(y_rims, 1).astype(jnp.bfloat16))
        return [
            (along_x[t * S : (t + 1) * S], along_y[:, t * S : (t + 1) * S]) for t in range(2)
        ]

    return level


def flow_of(flow, k):
    u = flow[k, :S].astype(jnp.float32)
    v = flow[k, S : 2 * S].astype(jnp.float32)
    return u, v, flow[k, 2 * S : 2 * S + 16].astype(jnp.float32)[:1]


def inner_change(u, v, mixing, x_ahead, x_behind, y_ahead, y_behind, curve):
    carry = u * jnp.where(u >= 0, x_ahead, x_behind) + v * jnp.where(v >= 0, y_ahead, y_behind)
    return mixing * curve - carry * (1.0 / 60.0)


def rim_change(u, v, mixing, x, y):
    x_part = mixing * x[:, 2 * S :] - u * jnp.where(u >= 0, x[:, :S], x[:, S : 2 * S]) * (1.0 / 60.0)

    def ends(first, at):
        w = v[at : at + 8]
        slope = jnp.where(w >= 0, y[first : first + 8], y[16 + first : 24 + first])
        return x_part[at : at + 8] + (
            mixing * y[32 + first : 40 + first] - w * slope * (1.0 / 60.0)
        )

    return jnp.concatenate([ends(0, 0), x_part[8 : S - 8], ends(8, S - 8)], 0)


def wet_of(levels, k):
    return levels[k : k + 1]


def lift_of(levels, k):
    return levels[LEVELS + k : LEVELS + k + 1]


def section_kernel(start, flow, levels, neighbours, mate, own, other, section, rims_out):
    tile = lax.axis_index("tile")
    near = beside(neighbours, tile)
    level = rim_sums(near, tile, (mate, own, other))
    rim_parts = {}

    def emit(p, x, y, z):
        k = p % LEVELS
        u, v, mixing = flow_of(flow, k)
        if p < LEVELS:
            rim_parts[p], rim_parts[p + LEVELS] = level(k)
        curve = x[:, 2 * S :] + y[2 * S :]
        change = inner_change(
            u, v, mixing, x[:, :S], x[:, S : 2 * S], y[:S], y[S : 2 * S], curve
        )
        change = change + rim_change(u, v, mixing, *rim_parts[p])
        section[p] = start[p] + (wet_of(levels, k) * change + lift_of(levels, k) * z)

    inner_sums(lambda p: start[p], emit)
    rims(lambda p: section[p], near[1] >= 0, tile, rims_out)


def inner_kernel(start, section, flow, levels, after, out):
    def emit(p, x, y, z):
        k = p % LEVELS
        u, v, mixing = flow_of(flow, k)
        curve = x[:, 2 * S :] + y[2 * S :]
        change = inner_change(
            u, v, mixing, x[:, :S], x[:, S : 2 * S], y[:S], y[S : 2 * S], curve
        )
        change = wet_of(levels, k) * change + lift_of(levels, k) * z
        out[p] = 0.5 * (start[p] + section[p] + change)

    inner_sums(lambda p: section[p], emit)


def last_kernel(inner, flow, levels, neighbours, mate, own, other, out, held, sent):
    tile = lax.axis_index("tile")
    near = beside(neighbours, tile)
    level = rim_sums(near, tile, (mate, own, other))
    copies = []
    for k in range(LEVELS):
        u, v, mixing = flow_of(flow, k)
        for t, (x, y) in enumerate(level(k)):
            p = k + t * LEVELS
            change = rim_change(u, v, mixing, x, y)
            held[p] = inner[p] + (0.5 * wet_of(levels, k)) * change
            copies.append(pltpu.make_async_copy(held.at[p], out.at[p], sent.at[p]))
            copies[-1].start()
    for copy in copies:
        copy.wait()


VMEM = pl.BlockSpec(memory_space=pltpu.VMEM)
SMEM = pl.BlockSpec(memory_space=pltpu.SMEM)
HBM = pl.BlockSpec(memory_space=pltpu.HBM)
ANY = pl.BlockSpec(memory_space=pl.ANY)
PARAMS = pltpu.CompilerParams(vmem_limit_bytes=24 * 1024 * 1024)
COST = pl.CostEstimate(flops=2 * 10**9, bytes_accessed=8 * 10**6, transcendentals=0)
FIELD = pltpu.VMEM((2 * LEVELS, S, S), jnp.float32)
RIMS = pltpu.VMEM((3, S // 2, S), jnp.bfloat16)


def across(mate, blocks):
    return lax.ppermute(jnp.concatenate([mate[:2], blocks[2:]], 0), "tile", ACROSS)


def local(
    tracers, east_velocity, north_velocity, diffusivity, vertical_diffusivity, depths, neighbours
):
    planes = 2 * LEVELS
    neighbours = neighbours.T
    inputs = (
        tracers.reshape(planes, S, S),
        east_velocity.reshape(S, S),
        north_velocity.reshape(S, S),
        diffusivity,
        depths,
        neighbours,
        vertical_diffusivity,
    )
    flow, blocks, start, levels = pl.pallas_call(
        first_kernel,
        out_shape=[
            pltpu.VMEM((LEVELS, 2 * S + 16, S), jnp.bfloat16),
            RIMS,
            FIELD,
            pltpu.VMEM((2 * LEVELS, S), jnp.float32),
        ],
        in_specs=[HBM] * 3 + [VMEM] + [HBM] * 3,
        out_specs=[VMEM] * 4,
        scratch_shapes=[
            pltpu.VMEM((planes, S, S), jnp.float32),
            pltpu.VMEM((S, S), jnp.bfloat16),
            pltpu.VMEM((S, S), jnp.bfloat16),
            pltpu.SMEM((TILES,), jnp.int32),
            pltpu.SMEM((4, TILES), jnp.int32),
            pltpu.SMEM((LEVELS,), jnp.float32),
            pltpu.SemaphoreType.DMA((6,)),
        ],
        compiler_params=PARAMS,
        name="rims",
    )(*(x if x is diffusivity else pltpu.with_memory_space_constraint(x, pltpu.HBM) for x in inputs))
    mate = lax.ppermute(blocks, "tile", MATES)
    flow = lax.all_to_all(flow, "tracer", 0, 0)
    own = across(mate, blocks)
    other = lax.ppermute(own, "tile", MATES)
    section, blocks = pl.pallas_call(
        section_kernel,
        out_shape=[FIELD, RIMS],
        in_specs=[VMEM] * 3 + [SMEM] + [VMEM] * 3,
        out_specs=[VMEM] * 2,
        compiler_params=PARAMS,
        name="section",
    )(start, flow, levels, neighbours, mate, own, other)
    mate = lax.ppermute(blocks, "tile", MATES)
    own = across(mate, blocks)
    inner = pl.pallas_call(
        inner_kernel,
        out_shape=FIELD,
        in_specs=[VMEM] * 4 + [ANY],
        out_specs=VMEM,
        compiler_params=PARAMS,
        cost_estimate=COST,
        name="inner",
    )(start, section, flow, levels, mate)
    own, inner = lax.optimization_barrier((own, inner))
    other = lax.ppermute(own, "tile", MATES)
    out = pl.pallas_call(
        last_kernel,
        out_shape=jax.ShapeDtypeStruct((planes, S, S), jnp.float32),
        in_specs=[VMEM] * 3 + [SMEM] + [VMEM] * 3,
        out_specs=HBM,
        scratch_shapes=[
            pltpu.VMEM((planes, S, S), jnp.float32),
            pltpu.SemaphoreType.DMA((planes,)),
        ],
        compiler_params=PARAMS,
        name="transported",
    )(inner, flow, levels, neighbours, mate, own, other)
    return out.reshape(tracers.shape)


def solution(mesh):
    return jax.shard_map(
        local,
        mesh=mesh,
        in_specs=(
            P("tracer", "tile", None, None, None),
            P("tile", "tracer", None, None),
            P("tile", "tracer", None, None),
            P("tile", "tracer"),
            P(),
            P(),
            P(),
        ),
        out_specs=P("tracer", "tile", None, None, None),
        check_vma=False,
    )
```

time: 43.1 us -> 38.7 us (0.90)
  local copies, waits for them, and re-layouts: 1.39 us -> 0.02 us
  Pallas kernels: 9.57 us -> 8.28 us
  waiting for transfers between devices: 10.9 us -> 9.69 us
  starting transfers between devices: 20.2 us -> 19.7 us
    unnamed x11 -> x2, local copies, waits for them, and re-layouts: 1.38 us -> 0.01 us
    pallas_call x3 -> x4, Pallas kernels: 9.57 us -> 8.28 us  [the longest x1 2.49 us: local(): pl.pallas_call(section_kernel, out_shape=[FIELD, RIMS], in_specs=[VMEM] *...]
    ppermute x6, waiting for transfers between devices: 10.9 us -> 9.69 us  [the longest x2 5.28 us: across(): lax.ppermute(jnp.concatenate([mate[:2], blocks[2:]], 0), 'tile', ACROSS)]
  transfers between devices with their start and end apart: 7 -> 7, of which waited for: 6 -> 6; matrix products, arithmetic and copies ran while one was open for 0% -> 0% of each run, Pallas kernels for 0% -> 4%
where the time goes in v1:
time: 38.7 us; the launch traced here: 38.4 us
  starting transfers between devices  19.7 us (51%)
  waiting for transfers between devices  9.69 us (25%)
  Pallas kernels  8.28 us (21%)
  between operations  0.71 us (2%)
    ppermute x2, starting transfers between devices, across(): lax.ppermute(jnp.concatenate([mate[:2], blocks[2:]], 0), 'tile', ACROSS)  12.5 us
    all_to_all x1, starting transfers between devices, local(): flow = lax.all_to_all(flow, 'tracer', 0, 0)  5.72 us
    ppermute x2, waiting for transfers between devices, across(): lax.ppermute(jnp.concatenate([mate[:2], blocks[2:]], 0), 'tile', ACROSS)  5.28 us
    pallas_call x1, Pallas kernels, local(): pl.pallas_call(section_kernel, out_shape=[FIELD, RIMS], in_specs=[VMEM] *...  2.49 us
    ppermute x2, waiting for transfers between devices, local(): other = lax.ppermute(own, 'tile', MATES)  2.46 us
    pallas_call x1, Pallas kernels, local(): pl.pallas_call(first_kernel, out_shape=[pltpu.VMEM((LEVELS, 2 * S + 16, S...  2.2 us
    pallas_call x1, Pallas kernels, local(): pl.pallas_call(last_kernel, out_shape=jax.ShapeDtypeStruct((planes, S, S)...  2.05 us
    ppermute x2, waiting for transfers between devices, local(): mate = lax.ppermute(blocks, 'tile', MATES)  1.95 us
  transfers between devices with their start and end apart: 7, of which 6 were waited for; matrix products, arithmetic and copies ran while one was open for 0% of the time, Pallas kernels for 4%

profile of v1, /device:TPU:15, one launch (start us, length us, event | category | flops | bytes accessed | tf_op | source)
XLA Modules:
  0.0 38.4 jit_solution(8378346256523770636)
XLA Ops:
  0.7 2.2 %rims.1 = (bf16[8,272,128]{2,1,0:T(8,128)(2,1)}, bf16[3,64,128]{2,1,0:T(8,128)(2,1)S(1)}, f32[16,128,128]{2,1,0:T(8,128)S(1)}, f32[16,128]{1,0:T(8,128)S(1)}) custom-call(f32[16,128,128]{2,1,0:T(8,128)} %bitcast.10, bf16[128,128]{1,0:T(8,128)(2,1)} %bitcast.11, bf16[128,128]{1,0:T(8,128)(2,1)} %bitcast.12, bf16[1,1]{1,0:T(2,128)(2,1)S(6)} %copy.9.mixing, ...), custom_call_target="tpu_custom_call" | custom-call | tf_op jit(solution)/shard_map/rims/pallas_call | solution.py:317
  2.9 5.7 %all-to-all-start = ((bf16[8,272,128]{2,1,0:T(8,128)(2,1)}), bf16[8,272,128]{2,1,0:T(8,128)(2,1)S(1)}, u32[]{:S(2)}, u32[]{:S(2)}) async-start(bf16[8,272,128]{2,1,0:T(8,128)(2,1)} %get-tuple-element.14), calls=%async_computation | async-start | bytes 1114112 | tf_op jit(solution)/shard_map/all_to_all | solution.py:340
  8.6 1.2 %collective-permute-start = (bf16[3,64,128]{2,1,0:T(8,128)(2,1)S(1)}, bf16[3,64,128]{2,1,0:T(8,128)(2,1)S(1)}, u32[]{:S(2)}, u32[]{:S(2)}) collective-permute-start(bf16[3,64,128]{2,1,0:T(8,128)(2,1)S(1)} %get-tuple-element.16), channel_id=1, source_target_pairs={{0,8},{8,0},{16,24},{24,16},{32,40},{40,32},{48,56},{56,48},{64,72... | collective-permute-start | bytes 147464 | tf_op jit(solution)/shard_map/ppermute | solution.py:339
  9.8 0.9 %collective-permute-done.mate = bf16[3,64,128]{2,1,0:T(8,128)(2,1)S(1)} collective-permute-done((bf16[3,64,128]{2,1,0:T(8,128)(2,1)S(1)}, bf16[3,64,128]{2,1,0:T(8,128)(2,1)S(1)}, u32[]{:S(2)}, u32[]{:S(2)}) %collective-permute-start) | collective-permute-done | bytes 49184 | tf_op jit(solution)/shard_map/ppermute | solution.py:339
  10.7 0.0 copy-start
  10.7 7.5 %collective-permute-start.1 = (bf16[3,64,128]{2,1,0:T(8,128)(2,1)S(1)}, bf16[3,64,128]{2,1,0:T(8,128)(2,1)S(1)}, u32[]{:S(2)}, u32[]{:S(2)}) collective-permute-start(bf16[3,64,128]{2,1,0:T(8,128)(2,1)S(1)} %pad_maximum_fusion), channel_id=1, source_target_pairs={{0,24},{16,40},{32,56},{48,72},{64,88},{80,104},{96,120},{112,136}... | collective-permute-start | bytes 147464 | tf_op jit(solution)/shard_map/ppermute | solution.py:300
  18.3 3.4 %collective-permute-done.1.own = bf16[3,64,128]{2,1,0:T(8,128)(2,1)S(1)} collective-permute-done((bf16[3,64,128]{2,1,0:T(8,128)(2,1)S(1)}, bf16[3,64,128]{2,1,0:T(8,128)(2,1)S(1)}, u32[]{:S(2)}, u32[]{:S(2)}) %collective-permute-start.1) | collective-permute-done | bytes 49184 | tf_op jit(solution)/shard_map/ppermute | solution.py:300
  21.7 0.0 collective-permute-start.2
  21.7 1.2 %collective-permute-done.2.other = bf16[3,64,128]{2,1,0:T(8,128)(2,1)S(1)} collective-permute-done((bf16[3,64,128]{2,1,0:T(8,128)(2,1)S(1)}, bf16[3,64,128]{2,1,0:T(8,128)(2,1)S(1)}, u32[]{:S(2)}, u32[]{:S(2)}) %collective-permute-start.2) | collective-permute-done | bytes 49184 | tf_op jit(solution)/shard_map/ppermute | solution.py:342
  22.9 0.0 all-to-all-done.flow
  22.9 0.0 copy-done
  22.9 2.5 %section.1 = (f32[16,128,128]{2,1,0:T(8,128)S(1)}, bf16[3,64,128]{2,1,0:T(8,128)(2,1)S(1)}) custom-call(f32[16,128,128]{2,1,0:T(8,128)S(1)} %get-tuple-element.13.start, bf16[8,272,128]{2,1,0:T(8,128)(2,1)S(1)} %all-to-all-done.flow, f32[16,128]{1,0:T(8,128)S(1)} %get-tuple-element.15.levels, s32[4,32]{1,0:T(4,128)S(1)} %bitcast.8, ...), custom_call_target="tpu_custom_call" | custom-call | tf_op jit(solution)/shard_map/section/pallas_call | solution.py:343
  25.4 0.2 collective-permute-start.3
  25.7 1.1 %collective-permute-done.3.after.mate = bf16[3,64,128]{2,1,0:T(8,128)(2,1)S(1)} collective-permute-done((bf16[3,64,128]{2,1,0:T(8,128)(2,1)S(1)}, bf16[3,64,128]{2,1,0:T(8,128)(2,1)S(1)}, u32[]{:S(2)}, u32[]{:S(2)}) %collective-permute-start.3) | collective-permute-done | bytes 49184 | tf_op jit(solution)/shard_map/ppermute | solution.py:351
  26.7 5.0 %collective-permute-start.4 = (bf16[3,64,128]{2,1,0:T(8,128)(2,1)S(1)}, bf16[3,64,128]{2,1,0:T(8,128)(2,1)S(1)}, u32[]{:S(2)}, u32[]{:S(2)}) collective-permute-start(bf16[3,64,128]{2,1,0:T(8,128)(2,1)S(1)} %pad_maximum_fusion.1), channel_id=1, source_target_pairs={{0,24},{16,40},{32,56},{48,72},{64,88},{80,104},{96,120},{112,136}... | collective-permute-start | bytes 147464 | tf_op jit(solution)/shard_map/ppermute | solution.py:300
  31.7 1.5 %inner.1 = f32[16,128,128]{2,1,0:T(8,128)S(1)} custom-call(f32[16,128,128]{2,1,0:T(8,128)S(1)} %get-tuple-element.13.start, f32[16,128,128]{2,1,0:T(8,128)S(1)} %get-tuple-element.18.section, bf16[8,272,128]{2,1,0:T(8,128)(2,1)S(1)} %all-to-all-done.flow, f32[16,128]{1,0:T(8,128)S(1)} %get-tuple-element.15.levels, ...), custom_call_target="tpu_custom_call" | custom-call | flops 2000000000 | bytes 8000000 | tf_op jit(solution)/shard_map/inner/pallas_call | solution.py:353
  33.3 1.9 %collective-permute-done.4.own = bf16[3,64,128]{2,1,0:T(8,128)(2,1)S(1)} collective-permute-done((bf16[3,64,128]{2,1,0:T(8,128)(2,1)S(1)}, bf16[3,64,128]{2,1,0:T(8,128)(2,1)S(1)}, u32[]{:S(2)}, u32[]{:S(2)}) %collective-permute-start.4) | collective-permute-done | bytes 49184 | tf_op jit(solution)/shard_map/ppermute | solution.py:300
  35.2 0.0 collective-permute-start.5
  35.2 1.2 %collective-permute-done.5.other = bf16[3,64,128]{2,1,0:T(8,128)(2,1)S(1)} collective-permute-done((bf16[3,64,128]{2,1,0:T(8,128)(2,1)S(1)}, bf16[3,64,128]{2,1,0:T(8,128)(2,1)S(1)}, u32[]{:S(2)}, u32[]{:S(2)}) %collective-permute-start.5) | collective-permute-done | bytes 49184 | tf_op jit(solution)/shard_map/ppermute | solution.py:363
  36.4 2.1 %transported.1 = f32[16,128,128]{2,1,0:T(8,128)} custom-call(f32[16,128,128]{2,1,0:T(8,128)S(1)} %inner.1, bf16[8,272,128]{2,1,0:T(8,128)(2,1)S(1)} %all-to-all-done.flow, f32[16,128]{1,0:T(8,128)S(1)} %get-tuple-element.15.levels, s32[4,32]{1,0:T(4,128)S(1)} %bitcast.9, bf16[3,64,128]{2,1,0:T(8,128)(2,1)S(1)} %collective-permute-done.3.after.mate, ...), custom_call_target="tpu_custom_call" | custom-call | tf_op jit(solution)/shard_map/transported/pallas_call | solution.py:364
  (6 shorter events, 0.0 us)
Async XLA Ops:
  2.9 20.0 %all-to-all-start = ((bf16[8,272,128]{2,1,0:T(8,128)(2,1)}), bf16[8,272,128]{2,1,0:T(8,128)(2,1)S(1)}, u32[]{:S(2)}, u32[]{:S(2)}) async-start(bf16[8,272,128]{2,1,0:T(8,128)(2,1)} %get-tuple-element.14), calls=%async_computation | async-start | bytes 1114112 | tf_op jit(solution)/shard_map/all_to_all | solution.py:340
  8.6 2.1 %collective-permute-start = (bf16[3,64,128]{2,1,0:T(8,128)(2,1)S(1)}, bf16[3,64,128]{2,1,0:T(8,128)(2,1)S(1)}, u32[]{:S(2)}, u32[]{:S(2)}) collective-permute-start(bf16[3,64,128]{2,1,0:T(8,128)(2,1)S(1)} %get-tuple-element.16), channel_id=1, source_target_pairs={{0,8},{8,0},{16,24},{24,16},{32,40},{40,32},{48,56},{56,48},{64,72... | collective-permute-start | bytes 147464 | tf_op jit(solution)/shard_map/ppermute | solution.py:339
  10.7 12.2 %copy-start = (s32[32,4]{0,1:T(4,128)S(1)}, s32[32,4]{0,1:T(4,128)}, u32[]{:S(2)}) copy-start(s32[32,4]{0,1:T(4,128)} %param.13) | copy-start | bytes 1540
  10.7 10.9 %collective-permute-start.1 = (bf16[3,64,128]{2,1,0:T(8,128)(2,1)S(1)}, bf16[3,64,128]{2,1,0:T(8,128)(2,1)S(1)}, u32[]{:S(2)}, u32[]{:S(2)}) collective-permute-start(bf16[3,64,128]{2,1,0:T(8,128)(2,1)S(1)} %pad_maximum_fusion), channel_id=1, source_target_pairs={{0,24},{16,40},{32,56},{48,72},{64,88},{80,104},{96,120},{112,136}... | collective-permute-start | bytes 147464 | tf_op jit(solution)/shard_map/ppermute | solution.py:300
  21.7 1.2 %collective-permute-start.2 = (bf16[3,64,128]{2,1,0:T(8,128)(2,1)S(1)}, bf16[3,64,128]{2,1,0:T(8,128)(2,1)S(1)}, u32[]{:S(2)}, u32[]{:S(2)}) collective-permute-start(bf16[3,64,128]{2,1,0:T(8,128)(2,1)S(1)} %collective-permute-done.1.own), channel_id=1, source_target_pairs={{0,8},{8,0},{16,24},{24,16},{32,40},{40,32},{48,56},{56,48},{64,72... | collective-permute-start | bytes 147464 | tf_op jit(solution)/shard_map/ppermute | solution.py:342
  25.4 1.3 %collective-permute-start.3 = (bf16[3,64,128]{2,1,0:T(8,128)(2,1)S(1)}, bf16[3,64,128]{2,1,0:T(8,128)(2,1)S(1)}, u32[]{:S(2)}, u32[]{:S(2)}) collective-permute-start(bf16[3,64,128]{2,1,0:T(8,128)(2,1)S(1)} %get-tuple-element.17), channel_id=1, source_target_pairs={{0,8},{8,0},{16,24},{24,16},{32,40},{40,32},{48,56},{56,48},{64,72... | collective-permute-start | bytes 147464 | tf_op jit(solution)/shard_map/ppermute | solution.py:351
  26.7 8.4 %collective-permute-start.4 = (bf16[3,64,128]{2,1,0:T(8,128)(2,1)S(1)}, bf16[3,64,128]{2,1,0:T(8,128)(2,1)S(1)}, u32[]{:S(2)}, u32[]{:S(2)}) collective-permute-start(bf16[3,64,128]{2,1,0:T(8,128)(2,1)S(1)} %pad_maximum_fusion.1), channel_id=1, source_target_pairs={{0,24},{16,40},{32,56},{48,72},{64,88},{80,104},{96,120},{112,136}... | collective-permute-start | bytes 147464 | tf_op jit(solution)/shard_map/ppermute | solution.py:300
  35.2 1.2 %collective-permute-start.5 = (bf16[3,64,128]{2,1,0:T(8,128)(2,1)S(1)}, bf16[3,64,128]{2,1,0:T(8,128)(2,1)S(1)}, u32[]{:S(2)}, u32[]{:S(2)}) collective-permute-start(bf16[3,64,128]{2,1,0:T(8,128)(2,1)S(1)} %collective-permute-done.4.own), channel_id=1, source_target_pairs={{0,8},{8,0},{16,24},{24,16},{32,40},{40,32},{48,56},{56,48},{64,72... | collective-permute-start | bytes 147464 | tf_op jit(solution)/shard_map/ppermute | solution.py:363

commit v2 on v1

--- a/solution.py
+++ b/solution.py
@@ -14,7 +14,12 @@
 BANDS = (AHEAD, BEHIND, CURVE)
 
 MATES = [(s, s ^ 1) for s in range(TILES)]
-ACROSS = [(s, s + 3) for s in range(0, TILES - 3, 2)] + [(s + 3, s) for s in range(0, TILES - 3, 2)]
+PAIRS = [(s, s + 2) for s in range(TILES - 2) if s % 4 in (0, 3)]
+ACROSS = PAIRS + [(t, s) for s, t in PAIRS]
+
+
+def looks_up(tile):
+    return (tile % 4 == 0) | (tile % 4 == 3)
 
 
 def beside(neighbours, tile):
@@ -59,10 +64,10 @@
         south.append(jnp.where(low, first[:8], pltpu.roll(second[:8], 4, 0)))
         north.append(jnp.where(low, pltpu.roll(first[S - 8 :], 4, 0), second[S - 8 :]))
     south, north = jnp.concatenate(south, 0), jnp.concatenate(north, 0)
-    even = tile % 2 == 0
+    up = looks_up(tile)
     out[0] = x_rim.astype(jnp.bfloat16)
-    out[1] = jnp.where(even, south, north).astype(jnp.bfloat16)
-    out[2] = jnp.where(even, north, south).astype(jnp.bfloat16)
+    out[1] = jnp.where(up, south, north).astype(jnp.bfloat16)
+    out[2] = jnp.where(up, north, south).astype(jnp.bfloat16)
 
 
 def first_kernel(
@@ -129,18 +134,24 @@
 def ghosts(near, tile, received):
     gx, gs, gn = (jnp.zeros((S // 2, S), jnp.float32) for _ in range(3))
     mate, own, other = received
-    toward = jnp.where(tile % 2 == 0, 1, -1)
-    for steps, x_block, y_block in (
-        (1, mate.at[0], mate.at[2]),
-        (2, None, own.at[1]),
-        (-1, other.at[0], other.at[1]),
-        (-2, None, other.at[2]),
-    ):
-        slot = tile + steps * toward
-        if x_block is not None:
+    chip = tile // 2
+    for steps in (-2, -1, 1, 2):
+        slot = tile + steps
+        from_chip = (tile + 2 * TILES + steps) // 2 - TILES
+        is_mate = from_chip == chip
+        is_own = (from_chip > chip) == looks_up(tile)
+        pair = jnp.minimum(from_chip, chip)
+        y_at = jnp.where((slot - pair) % 2 == 0, 2, 1)
+        if abs(steps) == 1:
             in_row = (slot == near[0]) | (slot == near[1])
-            gx = jnp.where(in_row, x_block[...].astype(jnp.float32), gx)
-        block = y_block[...].astype(jnp.float32)
+            block = jnp.where(is_own, own[0], other[0])
+            block = jnp.where(is_mate, mate[0], block)
+            gx = jnp.where(in_row, block.astype(jnp.float32), gx)
+            mate_y = jnp.where(tile % 4 < 2, mate[2], mate[1])
+            block = jnp.where(is_mate, mate_y, jnp.where(is_own, own[y_at], other[y_at]))
+        else:
+            block = jnp.where(is_own, own[y_at], other[y_at])
+        block = block.astype(jnp.float32)
         gs = jnp.where(slot == near[2], block, gs)
         gn = jnp.where(slot == near[3], block, gn)
     return jnp.concatenate([gx, pltpu.roll(gx, S // 2, 1)], 0), gs, gn
@@ -297,7 +308,9 @@
 
 
 def across(mate, blocks):
-    return lax.ppermute(jnp.concatenate([mate[:2], blocks[2:]], 0), "tile", ACROSS)
+    tile = lax.axis_index("tile")
+    x_rim = jnp.where(tile % 4 < 2, mate[:1], blocks[:1])
+    return lax.ppermute(jnp.concatenate([x_rim, mate[1:2], blocks[2:]], 0), "tile", ACROSS)
 
 
 def local(

time: 38.7 us -> 37.3 us (0.964)
  waiting for transfers between devices: 9.69 us -> 8.23 us
    ppermute x2, waiting for transfers between devices: 5.28 us -> 3.82 us  [across(): lax.ppermute(jnp.concatenate([x_rim, mate[1:2], blocks[2:]], 0), 'tile',...]
where the time goes in v2:
time: 37.3 us; the launch traced here: 36.9 us
  starting transfers between devices  19.6 us (53%)
  Pallas kernels  8.31 us (22%)
  waiting for transfers between devices  8.23 us (22%)
  between operations  0.71 us (2%)
    ppermute x2, starting transfers between devices, across(): lax.ppermute(jnp.concatenate([x_rim, mate[1:2], blocks[2:]], 0), 'tile',...  12.4 us
    all_to_all x1, starting transfers between devices, local(): flow = lax.all_to_all(flow, 'tracer', 0, 0)  5.72 us
    ppermute x2, waiting for transfers between devices, across(): lax.ppermute(jnp.concatenate([x_rim, mate[1:2], blocks[2:]], 0), 'tile',...  3.82 us
    pallas_call x1, Pallas kernels, local(): pl.pallas_call(section_kernel, out_shape=[FIELD, RIMS], in_specs=[VMEM] *...  2.49 us
    ppermute x2, waiting for transfers between devices, local(): other = lax.ppermute(own, 'tile', MATES)  2.46 us
    pallas_call x1, Pallas kernels, local(): pl.pallas_call(first_kernel, out_shape=[pltpu.VMEM((LEVELS, 2 * S + 16, S...  2.21 us
    pallas_call x1, Pallas kernels, local(): pl.pallas_call(last_kernel, out_shape=jax.ShapeDtypeStruct((planes, S, S)...  2.07 us
    ppermute x2, waiting for transfers between devices, local(): mate = lax.ppermute(blocks, 'tile', MATES)  1.95 us
  transfers between devices with their start and end apart: 7, of which 6 were waited for; matrix products, arithmetic and copies ran while one was open for 0% of the time, Pallas kernels for 4%

profile of v2, /device:TPU:15, one launch (start us, length us, event | category | flops | bytes accessed | tf_op | source)
XLA Modules:
  0.0 36.9 jit_solution(3709272836687850760)
XLA Ops:
  0.7 2.2 %rims.1 = (bf16[8,272,128]{2,1,0:T(8,128)(2,1)}, bf16[3,64,128]{2,1,0:T(8,128)(2,1)S(1)}, f32[16,128,128]{2,1,0:T(8,128)S(1)}, f32[16,128]{1,0:T(8,128)S(1)}) custom-call(f32[16,128,128]{2,1,0:T(8,128)} %bitcast.10, bf16[128,128]{1,0:T(8,128)(2,1)} %bitcast.11, bf16[128,128]{1,0:T(8,128)(2,1)} %bitcast.12, bf16[1,1]{1,0:T(2,128)(2,1)S(6)} %copy.9.mixing, ...), custom_call_target="tpu_custom_call" | custom-call | tf_op jit(solution)/shard_map/rims/pallas_call | solution.py:330
  2.9 5.7 %all-to-all-start = ((bf16[8,272,128]{2,1,0:T(8,128)(2,1)}), bf16[8,272,128]{2,1,0:T(8,128)(2,1)S(1)}, u32[]{:S(2)}, u32[]{:S(2)}) async-start(bf16[8,272,128]{2,1,0:T(8,128)(2,1)} %get-tuple-element.14), calls=%async_computation | async-start | bytes 1114112 | tf_op jit(solution)/shard_map/all_to_all | solution.py:353
  8.6 1.2 %collective-permute-start = (bf16[3,64,128]{2,1,0:T(8,128)(2,1)S(1)}, bf16[3,64,128]{2,1,0:T(8,128)(2,1)S(1)}, u32[]{:S(2)}, u32[]{:S(2)}) collective-permute-start(bf16[3,64,128]{2,1,0:T(8,128)(2,1)S(1)} %get-tuple-element.16), channel_id=1, source_target_pairs={{0,8},{8,0},{16,24},{24,16},{32,40},{40,32},{48,56},{56,48},{64,72... | collective-permute-start | bytes 147464 | tf_op jit(solution)/shard_map/ppermute | solution.py:352
  9.8 0.9 %collective-permute-done.mate = bf16[3,64,128]{2,1,0:T(8,128)(2,1)S(1)} collective-permute-done((bf16[3,64,128]{2,1,0:T(8,128)(2,1)S(1)}, bf16[3,64,128]{2,1,0:T(8,128)(2,1)S(1)}, u32[]{:S(2)}, u32[]{:S(2)}) %collective-permute-start) | collective-permute-done | bytes 49184 | tf_op jit(solution)/shard_map/ppermute | solution.py:352
  10.7 0.0 copy-start
  10.8 7.3 %collective-permute-start.1 = (bf16[3,64,128]{2,1,0:T(8,128)(2,1)S(1)}, bf16[3,64,128]{2,1,0:T(8,128)(2,1)S(1)}, u32[]{:S(2)}, u32[]{:S(2)}) collective-permute-start(bf16[3,64,128]{2,1,0:T(8,128)(2,1)S(1)} %pad_maximum_fusion), channel_id=1, source_target_pairs={{0,16},{24,40},{32,48},{56,72},{64,80},{88,104},{96,112},{120,136}... | collective-permute-start | bytes 147464 | tf_op jit(solution)/shard_map/ppermute | solution.py:313
  18.1 2.7 %collective-permute-done.1.own = bf16[3,64,128]{2,1,0:T(8,128)(2,1)S(1)} collective-permute-done((bf16[3,64,128]{2,1,0:T(8,128)(2,1)S(1)}, bf16[3,64,128]{2,1,0:T(8,128)(2,1)S(1)}, u32[]{:S(2)}, u32[]{:S(2)}) %collective-permute-start.1) | collective-permute-done | bytes 49184 | tf_op jit(solution)/shard_map/ppermute | solution.py:313
  20.7 0.0 collective-permute-start.2
  20.7 1.2 %collective-permute-done.2.other = bf16[3,64,128]{2,1,0:T(8,128)(2,1)S(1)} collective-permute-done((bf16[3,64,128]{2,1,0:T(8,128)(2,1)S(1)}, bf16[3,64,128]{2,1,0:T(8,128)(2,1)S(1)}, u32[]{:S(2)}, u32[]{:S(2)}) %collective-permute-start.2) | collective-permute-done | bytes 49184 | tf_op jit(solution)/shard_map/ppermute | solution.py:355
  22.0 0.0 all-to-all-done.flow
  22.0 0.0 copy-done
  22.0 2.5 %section.1 = (f32[16,128,128]{2,1,0:T(8,128)S(1)}, bf16[3,64,128]{2,1,0:T(8,128)(2,1)S(1)}) custom-call(f32[16,128,128]{2,1,0:T(8,128)S(1)} %get-tuple-element.13.start, bf16[8,272,128]{2,1,0:T(8,128)(2,1)S(1)} %all-to-all-done.flow, f32[16,128]{1,0:T(8,128)S(1)} %get-tuple-element.15.levels, s32[4,32]{1,0:T(4,128)S(1)} %bitcast.8, ...), custom_call_target="tpu_custom_call" | custom-call | tf_op jit(solution)/shard_map/section/pallas_call | solution.py:356
  24.5 0.2 collective-permute-start.3
  24.7 1.1 %collective-permute-done.3.after.mate = bf16[3,64,128]{2,1,0:T(8,128)(2,1)S(1)} collective-permute-done((bf16[3,64,128]{2,1,0:T(8,128)(2,1)S(1)}, bf16[3,64,128]{2,1,0:T(8,128)(2,1)S(1)}, u32[]{:S(2)}, u32[]{:S(2)}) %collective-permute-start.3) | collective-permute-done | bytes 49184 | tf_op jit(solution)/shard_map/ppermute | solution.py:364
  25.8 5.2 %collective-permute-start.4 = (bf16[3,64,128]{2,1,0:T(8,128)(2,1)S(1)}, bf16[3,64,128]{2,1,0:T(8,128)(2,1)S(1)}, u32[]{:S(2)}, u32[]{:S(2)}) collective-permute-start(bf16[3,64,128]{2,1,0:T(8,128)(2,1)S(1)} %pad_maximum_fusion.1), channel_id=1, source_target_pairs={{0,16},{24,40},{32,48},{56,72},{64,80},{88,104},{96,112},{120,136}... | collective-permute-start | bytes 147464 | tf_op jit(solution)/shard_map/ppermute | solution.py:313
  31.0 1.5 %inner.1 = f32[16,128,128]{2,1,0:T(8,128)S(1)} custom-call(f32[16,128,128]{2,1,0:T(8,128)S(1)} %get-tuple-element.13.start, f32[16,128,128]{2,1,0:T(8,128)S(1)} %get-tuple-element.18.section, bf16[8,272,128]{2,1,0:T(8,128)(2,1)S(1)} %all-to-all-done.flow, f32[16,128]{1,0:T(8,128)S(1)} %get-tuple-element.15.levels, ...), custom_call_target="tpu_custom_call" | custom-call | flops 2000000000 | bytes 8000000 | tf_op jit(solution)/shard_map/inner/pallas_call | solution.py:366
  32.5 1.1 %collective-permute-done.4.own = bf16[3,64,128]{2,1,0:T(8,128)(2,1)S(1)} collective-permute-done((bf16[3,64,128]{2,1,0:T(8,128)(2,1)S(1)}, bf16[3,64,128]{2,1,0:T(8,128)(2,1)S(1)}, u32[]{:S(2)}, u32[]{:S(2)}) %collective-permute-start.4) | collective-permute-done | bytes 49184 | tf_op jit(solution)/shard_map/ppermute | solution.py:313
  33.6 0.0 collective-permute-start.5
  33.6 1.2 %collective-permute-done.5.other = bf16[3,64,128]{2,1,0:T(8,128)(2,1)S(1)} collective-permute-done((bf16[3,64,128]{2,1,0:T(8,128)(2,1)S(1)}, bf16[3,64,128]{2,1,0:T(8,128)(2,1)S(1)}, u32[]{:S(2)}, u32[]{:S(2)}) %collective-permute-start.5) | collective-permute-done | bytes 49184 | tf_op jit(solution)/shard_map/ppermute | solution.py:376
  34.9 2.1 %transported.1 = f32[16,128,128]{2,1,0:T(8,128)} custom-call(f32[16,128,128]{2,1,0:T(8,128)S(1)} %inner.1, bf16[8,272,128]{2,1,0:T(8,128)(2,1)S(1)} %all-to-all-done.flow, f32[16,128]{1,0:T(8,128)S(1)} %get-tuple-element.15.levels, s32[4,32]{1,0:T(4,128)S(1)} %bitcast.9, bf16[3,64,128]{2,1,0:T(8,128)(2,1)S(1)} %collective-permute-done.3.after.mate, ...), custom_call_target="tpu_custom_call" | custom-call | tf_op jit(solution)/shard_map/transported/pallas_call | solution.py:377
  (4 shorter events, 0.0 us)
Async XLA Ops:
  2.9 19.1 %all-to-all-start = ((bf16[8,272,128]{2,1,0:T(8,128)(2,1)}), bf16[8,272,128]{2,1,0:T(8,128)(2,1)S(1)}, u32[]{:S(2)}, u32[]{:S(2)}) async-start(bf16[8,272,128]{2,1,0:T(8,128)(2,1)} %get-tuple-element.14), calls=%async_computation | async-start | bytes 1114112 | tf_op jit(solution)/shard_map/all_to_all | solution.py:353
  8.6 2.1 %collective-permute-start = (bf16[3,64,128]{2,1,0:T(8,128)(2,1)S(1)}, bf16[3,64,128]{2,1,0:T(8,128)(2,1)S(1)}, u32[]{:S(2)}, u32[]{:S(2)}) collective-permute-start(bf16[3,64,128]{2,1,0:T(8,128)(2,1)S(1)} %get-tuple-element.16), channel_id=1, source_target_pairs={{0,8},{8,0},{16,24},{24,16},{32,40},{40,32},{48,56},{56,48},{64,72... | collective-permute-start | bytes 147464 | tf_op jit(solution)/shard_map/ppermute | solution.py:352
  10.7 11.2 %copy-start = (s32[32,4]{0,1:T(4,128)S(1)}, s32[32,4]{0,1:T(4,128)}, u32[]{:S(2)}) copy-start(s32[32,4]{0,1:T(4,128)} %param.13) | copy-start | bytes 1540
  10.8 10.0 %collective-permute-start.1 = (bf16[3,64,128]{2,1,0:T(8,128)(2,1)S(1)}, bf16[3,64,128]{2,1,0:T(8,128)(2,1)S(1)}, u32[]{:S(2)}, u32[]{:S(2)}) collective-permute-start(bf16[3,64,128]{2,1,0:T(8,128)(2,1)S(1)} %pad_maximum_fusion), channel_id=1, source_target_pairs={{0,16},{24,40},{32,48},{56,72},{64,80},{88,104},{96,112},{120,136}... | collective-permute-start | bytes 147464 | tf_op jit(solution)/shard_map/ppermute | solution.py:313
  20.7 1.2 %collective-permute-start.2 = (bf16[3,64,128]{2,1,0:T(8,128)(2,1)S(1)}, bf16[3,64,128]{2,1,0:T(8,128)(2,1)S(1)}, u32[]{:S(2)}, u32[]{:S(2)}) collective-permute-start(bf16[3,64,128]{2,1,0:T(8,128)(2,1)S(1)} %collective-permute-done.1.own), channel_id=1, source_target_pairs={{0,8},{8,0},{16,24},{24,16},{32,40},{40,32},{48,56},{56,48},{64,72... | collective-permute-start | bytes 147464 | tf_op jit(solution)/shard_map/ppermute | solution.py:355
  24.5 1.3 %collective-permute-start.3 = (bf16[3,64,128]{2,1,0:T(8,128)(2,1)S(1)}, bf16[3,64,128]{2,1,0:T(8,128)(2,1)S(1)}, u32[]{:S(2)}, u32[]{:S(2)}) collective-permute-start(bf16[3,64,128]{2,1,0:T(8,128)(2,1)S(1)} %get-tuple-element.17), channel_id=1, source_target_pairs={{0,8},{8,0},{16,24},{24,16},{32,40},{40,32},{48,56},{56,48},{64,72... | collective-permute-start | bytes 147464 | tf_op jit(solution)/shard_map/ppermute | solution.py:364
  25.8 7.8 %collective-permute-start.4 = (bf16[3,64,128]{2,1,0:T(8,128)(2,1)S(1)}, bf16[3,64,128]{2,1,0:T(8,128)(2,1)S(1)}, u32[]{:S(2)}, u32[]{:S(2)}) collective-permute-start(bf16[3,64,128]{2,1,0:T(8,128)(2,1)S(1)} %pad_maximum_fusion.1), channel_id=1, source_target_pairs={{0,16},{24,40},{32,48},{56,72},{64,80},{88,104},{96,112},{120,136}... | collective-permute-start | bytes 147464 | tf_op jit(solution)/shard_map/ppermute | solution.py:313
  33.6 1.2 %collective-permute-start.5 = (bf16[3,64,128]{2,1,0:T(8,128)(2,1)S(1)}, bf16[3,64,128]{2,1,0:T(8,128)(2,1)S(1)}, u32[]{:S(2)}, u32[]{:S(2)}) collective-permute-start(bf16[3,64,128]{2,1,0:T(8,128)(2,1)S(1)} %collective-permute-done.4.own), channel_id=1, source_target_pairs={{0,8},{8,0},{16,24},{24,16},{32,40},{40,32},{48,56},{56,48},{64,72... | collective-permute-start | bytes 147464 | tf_op jit(solution)/shard_map/ppermute | solution.py:376

commit v3 on v2

v3 whole, which is shorter than its diff:
```python
import jax
import jax.numpy as jnp
from jax import lax
from jax.experimental import pallas as pl
from jax.experimental.pallas import tpu as pltpu
from jax.sharding import PartitionSpec as P

S = 128
LEVELS = 8
TILES = 32
AHEAD = (-2.0, 15.0, -60.0, 20.0, 30.0, -3.0, 0.0)
BEHIND = (0.0, 3.0, -30.0, -20.0, 60.0, -15.0, 2.0)
CURVE = (0.0, 0.0, 1.0, -2.0, 1.0, 0.0, 0.0)
BANDS = (AHEAD, BEHIND, CURVE)

MATES = [(s, s ^ 1) for s in range(TILES)]
PAIRS = [(s, s + 2) for s in range(TILES - 2) if s % 4 in (0, 3)]
ACROSS = PAIRS + [(t, s) for s, t in PAIRS]


def looks_up(tile):
    return (tile % 4 == 0) | (tile % 4 == 3)


def beside(neighbours, tile):
    row = [neighbours[e, tile] for e in range(4)]
    return [jnp.where(slot < 0, -9, slot) for slot in row]


def band(distance, coefficients):
    total = jnp.zeros(distance.shape, jnp.float32)
    for step, coefficient in zip(range(-3, 4), coefficients):
        if coefficient:
            total = jnp.where(distance == step, coefficient, total)
    return total


def iota(shape, dim):
    return lax.broadcasted_iota(jnp.int32, shape, dim)


def bands(distance, axis):
    return jnp.concatenate([band(distance, c) for c in BANDS], axis).astype(jnp.bfloat16)


def pack_rims(tile, x_rim, top, bottom, out):
    half = S // 2
    lane = iota((half, S), 1)
    x_rim = jnp.where(lane < half, x_rim[:half], pltpu.roll(x_rim[half:], half, 1))
    low = iota((8, S), 0) < 4
    south, north = [], []
    for p in range(0, 2 * LEVELS, 2):
        south.append(jnp.where(low, top(p), pltpu.roll(top(p + 1), 4, 0)))
        north.append(jnp.where(low, pltpu.roll(bottom(p), 4, 0), bottom(p + 1)))
    south, north = jnp.concatenate(south, 0), jnp.concatenate(north, 0)
    up = looks_up(tile)
    out[0] = x_rim.astype(jnp.bfloat16)
    out[1] = jnp.where(up, south, north).astype(jnp.bfloat16)
    out[2] = jnp.where(up, north, south).astype(jnp.bfloat16)


def rims(field, side_east, tile, out):
    lane = iota((S, S), 1)
    shift = jnp.where(side_east, 4, 0)
    x_rim = jnp.zeros((S, S), jnp.float32)
    for p in range(2 * LEVELS):
        x_rim = jnp.where(lane // 4 == p, pltpu.roll(field[p], shift + 4 * p, 1), x_rim)
    pack_rims(tile, x_rim, lambda p: field[p, :8], lambda p: field[p, S - 8 :], out)


def first_kernel(
    tracers_in,
    east_in,
    north_in,
    mixing,
    depths_in,
    neighbours_in,
    vertical_in,
    flow_out,
    rims_out,
    start_out,
    levels_out,
    tracers,
    east,
    north,
    depths,
    neighbours,
    vertical,
    block,
    arrived,
    sent,
):
    copies = [
        pltpu.make_async_copy(source, target, arrived.at[i])
        for i, (source, target) in enumerate(
            (
                (east_in, east),
                (north_in, north),
                (depths_in, depths),
                (neighbours_in, neighbours),
                (vertical_in, vertical),
                (tracers_in, tracers),
            )
        )
    ]
    for copy in copies:
        copy.start()
    for copy in copies[:2]:
        copy.wait()
    block[:S] = east[...]
    block[S : 2 * S] = north[...]
    last = jnp.broadcast_to(mixing[...].astype(jnp.float32), (16, S))
    block[2 * S :] = last.astype(jnp.bfloat16)
    leaving = [pltpu.make_async_copy(block, flow_out.at[j], sent.at[j]) for j in range(LEVELS)]
    for copy in leaving:
        copy.start()
    for copy in copies[2:]:
        copy.wait()
    tile = lax.axis_index("tile")
    depth = depths[tile]

    for k in range(LEVELS):
        wet = (k < depth).astype(jnp.float32)
        levels_out[k : k + 1] = jnp.full((1, S), wet, jnp.float32)
        levels_out[LEVELS + k : LEVELS + k + 1] = jnp.full((1, S), wet * vertical[k], jnp.float32)
    for p in range(2 * LEVELS):
        start_out[p] = tracers[p] * (p % LEVELS < depth).astype(jnp.float32)
    rims(start_out, neighbours[1, tile] >= 0, tile, rims_out)
    for copy in leaving:
        copy.wait()


def ghosts(near, tile, received):
    gx, gs, gn = (jnp.zeros((S // 2, S), jnp.float32) for _ in range(3))
    mate, own, other = received
    chip = tile // 2
    for steps in (-2, -1, 1, 2):
        slot = tile + steps
        from_chip = (tile + 2 * TILES + steps) // 2 - TILES
        is_mate = from_chip == chip
        is_own = (from_chip > chip) == looks_up(tile)
        pair = jnp.minimum(from_chip, chip)
        y_at = jnp.where((slot - pair) % 2 == 0, 2, 1)
        if abs(steps) == 1:
            in_row = (slot == near[0]) | (slot == near[1])
            block = jnp.where(is_own, own[0], other[0])
            block = jnp.where(is_mate, mate[0], block)
            gx = jnp.where(in_row, block.astype(jnp.float32), gx)
            mate_y = jnp.where(tile % 4 < 2, mate[2], mate[1])
            block = jnp.where(is_mate, mate_y, jnp.where(is_own, own[y_at], other[y_at]))
        else:
            block = jnp.where(is_own, own[y_at], other[y_at])
        block = block.astype(jnp.float32)
        gs = jnp.where(slot == near[2], block, gs)
        gn = jnp.where(slot == near[3], block, gn)
    return jnp.concatenate([gx, pltpu.roll(gx, S // 2, 1)], 0), gs, gn


def dot(a, b):
    return jnp.dot(a, b, preferred_element_type=jnp.float32)


def split(q):
    high = q.astype(jnp.bfloat16)
    return high, (q - high.astype(jnp.float32)).astype(jnp.bfloat16)


def inner_sums(values, right, left, emit):
    for k in range(LEVELS):
        pair = [values(k), values(k + LEVELS)]
        parts = [split(q) for q in pair]
        along_x = dot(jnp.concatenate([jnp.concatenate(q, 1) for q in parts], 0), right[...])
        along_y = dot(left[...], jnp.concatenate([jnp.concatenate(q, 0) for q in parts], 1))
        for t in range(2):
            z = second_difference(values, k + t * LEVELS)
            emit(k + t * LEVELS, along_x[t * S : (t + 1) * S], along_y[:, t * S : (t + 1) * S], z)


def second_difference(values, p):
    z = -2.0 * values(p)
    if p % LEVELS > 0:
        z = z + values(p - 1)
    if p % LEVELS < LEVELS - 1:
        z = z + values(p + 1)
    return z


def rim_changes(near, tile, received, flow, along, right_rim_packed, left_rim):
    gx, gs, gn = ghosts(near, tile, received)
    sums = dot(gx.astype(jnp.bfloat16), right_rim_packed[...])
    u = along[:S]
    change = carried(u, along[S : S + 1], sums[:, :S], sums[:, S : 2 * S], sums[:, 2 * S :])
    packed = along[S + 8 : S + 9] * change
    side_east = near[1] >= 0
    lane = iota((S, S), 1)
    window = lane - jnp.where(side_east, S - 8, 0)
    in_window = (window >= 0) & (window < 8)
    back = jnp.where(side_east, S - 8, S)

    def rows(p):
        return jnp.where(in_window, pltpu.roll(packed, back - 8 * p, 1), 0.0)

    sums_y = []
    for odd in range(2):
        y_rims = [
            jnp.concatenate([gs[8 * t : 8 * t + 8], gn[8 * t : 8 * t + 8]], 0)
            for t in range(LEVELS)
        ]
        sums_y.append(dot(left_rim[odd], jnp.concatenate(y_rims, 1).astype(jnp.bfloat16)))

    def ends(p):
        _, v, mixing = flow_of(flow, p % LEVELS)
        v = jnp.concatenate([v[:8], v[S - 8 :]], 0)
        y = sums_y[p % 2][:, S * (p // 2) : S * (p // 2 + 1)]
        return carried(v, mixing, y[:16], y[16:32], y[32:])

    return rows, ends


def add_ends(plane, ends):
    return jnp.concatenate(
        [plane[:8] + ends[:8], plane[8 : S - 8], plane[S - 8 :] + ends[8:]], 0
    )


def bands_kernel(
    start,
    neighbours,
    after,
    columns,
    right,
    left,
    right_rim,
    left_rim,
    right_packed,
    right_rim_packed,
    left_edge,
    left_rim_packed,
    repack,
):
    tile = lax.axis_index("tile")
    side_east = neighbours[1, tile] >= 0
    row, lane = iota((S, S), 0), iota((S, S), 1)
    own = bands(row - lane, 1)
    right[...] = jnp.concatenate([own, own], 0)
    own = bands(lane - row, 0)
    left[...] = jnp.concatenate([own, own], 1)
    base = jnp.where(side_east, S, -4)
    right_rim[...] = bands(row % 4 + base - lane, 1)
    own = bands(jnp.where(row // 8 == lane // 8, row % 8 - lane % 8, S), 1)
    right_packed[...] = jnp.concatenate([own, own], 0)
    base = jnp.where(side_east, 8, -4)
    right_rim_packed[...] = bands(
        jnp.where(row // 4 == lane // 8, row % 4 + base - lane % 8, S), 1
    )
    at = row % 8 - jnp.where(side_east, 4, 0)
    moves = (row // 8 == lane // 4) & (at == lane % 4)
    repack[...] = jnp.where(moves, 1.0, 0.0).astype(jnp.bfloat16)
    out = iota((16, 48), 0)
    out = jnp.where(out < 8, out, out + S - 16)
    column = iota((16, 48), 1)
    cell = column % 16
    same = jnp.where(cell < 8, cell, cell + S - 16)
    rim = jnp.where(cell < 8, cell % 4 - 4, cell % 4 + S)
    for odd in range(2):
        mine = jnp.where((cell // 4) % 2 == odd, rim, -2 * S)
        left_edge[odd] = bands(jnp.where(column < 32, same, mine) - out, 0)
        left_rim[odd] = bands(mine[:, :16] - out[:, :16], 0)
    cell = column[:, :16]
    both = jnp.where(cell < 4, cell - 4, jnp.where(cell < 8, cell + S - 4, -2 * S))
    left_rim_packed[...] = bands(both - out[:, :16], 0)
    packed = jnp.zeros((S, S), jnp.float32)
    shift = jnp.where(side_east, 8, 0)
    for p in range(2 * LEVELS):
        packed = jnp.where(lane // 8 == p, pltpu.roll(start[p], shift + 8 * p, 1), packed)
    columns[...] = packed


def flow_of(flow, k):
    u = flow[k, :S].astype(jnp.float32)
    v = flow[k, S : 2 * S].astype(jnp.float32)
    return u, v, flow[k, 2 * S : 2 * S + 16].astype(jnp.float32)[:1]


def inner_change(u, v, mixing, x_ahead, x_behind, y_ahead, y_behind, curve):
    carry = u * jnp.where(u >= 0, x_ahead, x_behind) + v * jnp.where(v >= 0, y_ahead, y_behind)
    return mixing * curve - carry * (1.0 / 60.0)


def carried(flow, mixing, ahead, behind, curve):
    return mixing * curve - flow * jnp.where(flow >= 0, ahead, behind) * (1.0 / 60.0)


def wet_of(levels, k):
    return levels[k : k + 1]


def lift_of(levels, k):
    return levels[LEVELS + k : LEVELS + k + 1]


def edge_kernel(
    start,
    columns,
    flow,
    levels,
    neighbours,
    mate,
    own,
    other,
    right,
    right_rim,
    left,
    right_packed,
    right_rim_packed,
    left_edge,
    left_rim_packed,
    repack,
    rims_out,
    along_out,
):
    tile = lax.axis_index("tile")
    near = beside(neighbours, tile)
    gx, gs, gn = ghosts(near, tile, (mate, own, other))
    planes = 2 * LEVELS

    shift = jnp.where(near[1] >= 0, 8, 0)
    block = iota((S, S), 1) // 8
    u_packed = jnp.zeros((S, S), jnp.float32)
    v_packed = jnp.zeros((S, S), jnp.float32)
    row_block = block[:1] % LEVELS
    mixing, wet, lift = (jnp.zeros((1, S), jnp.float32) for _ in range(3))
    for k in range(LEVELS):
        u, v, m = flow_of(flow, k)
        u_packed = jnp.where(block == k, pltpu.roll(u, shift + 8 * k, 1), u_packed)
        v_packed = jnp.where(block == k, pltpu.roll(v, shift + 8 * k, 1), v_packed)
        mixing = jnp.where(row_block == k, m, mixing)
        wet = jnp.where(row_block == k, wet_of(levels, k), wet)
        lift = jnp.where(row_block == k, lift_of(levels, k), lift)
    u_packed = jnp.where(block < LEVELS, u_packed, pltpu.roll(u_packed, S // 2, 1))
    v_packed = jnp.where(block < LEVELS, v_packed, pltpu.roll(v_packed, S // 2, 1))
    along_out[:S] = u_packed
    along_out[S : S + 8] = jnp.broadcast_to(mixing, (8, S))
    along_out[S + 8 :] = jnp.broadcast_to(wet, (8, S))
    low = iota((8, S), 0) < 4
    rim = jnp.zeros((8, S), jnp.float32)
    for p in range(planes):
        at = 8 * (p // 2)
        pair = (gs[at : at + 8], gn[at : at + 8])
        if p % 2:
            both = jnp.where(low, pltpu.roll(pair[0], 4, 0), pair[1])
        else:
            both = jnp.where(low, pair[0], pltpu.roll(pair[1], 4, 0))
        rim = jnp.where(block[:8] == p, pltpu.roll(both, shift + 8 * p, 1), rim)
    rim = jnp.concatenate([rim, jnp.zeros_like(rim)], 0).astype(jnp.bfloat16)
    q = columns[...]
    parts = split(q)
    x = dot(jnp.concatenate(parts, 1), right_packed[...])
    x = x + dot(gx.astype(jnp.bfloat16), right_rim_packed[...])
    y = dot(left[...], jnp.concatenate(parts, 0))
    y_rim = dot(left_rim_packed[...], rim)
    y = [
        jnp.concatenate(
            [
                y[i * S : i * S + 8] + y_rim[16 * i : 16 * i + 8],
                y[i * S + 8 : (i + 1) * S - 8],
                y[(i + 1) * S - 8 : (i + 1) * S] + y_rim[16 * i + 8 : 16 * i + 16],
            ],
            0,
        )
        for i in range(3)
    ]
    z = -2.0 * q
    z = z + jnp.where(block % LEVELS > 0, pltpu.roll(q, 8, 1), 0.0)
    z = z + jnp.where(block % LEVELS < LEVELS - 1, pltpu.roll(q, S - 8, 1), 0.0)
    change = inner_change(
        u_packed, v_packed, mixing, x[:, :S], x[:, S : 2 * S], y[0], y[1], x[:, 2 * S :] + y[2]
    )
    section = q + (wet * change + lift * z)
    x_rim = dot(section.astype(jnp.bfloat16), repack[...])

    def ends(a):
        return jnp.concatenate([a[:8], a[S - 8 :]], 0)

    values = [jnp.concatenate([start[p, :8], start[p, S - 8 :]], 0) for p in range(planes)]
    parts = [split(q) for q in values]
    gx_ends = ends(gx)
    lane_block = iota((16, S), 1) // 4
    x_rims = [jnp.where(lane_block == p, gx_ends, 0.0) for p in range(planes)]
    x = dot(jnp.concatenate([jnp.concatenate(q, 1) for q in parts], 0), right[...])
    x = x + dot(jnp.concatenate(x_rims, 0).astype(jnp.bfloat16), right_rim[...])
    ys = []
    for odd in range(2):
        sources = []
        for p in range(odd, planes, 2):
            at = 8 * (p // 2)
            y_rims = jnp.concatenate([gs[at : at + 8], gn[at : at + 8]], 0).astype(jnp.bfloat16)
            sources.append(jnp.concatenate([*parts[p], y_rims], 0))
        ys.append(dot(left_edge[odd], jnp.concatenate(sources, 1)))
    sections = []
    for p in range(planes):
        k = p % LEVELS
        u = ends(flow[k, :S].astype(jnp.float32))
        v = ends(flow[k, S : 2 * S].astype(jnp.float32))
        m = flow[k, 2 * S : 2 * S + 16].astype(jnp.float32)
        xp = x[16 * p : 16 * p + 16]
        yp = ys[p % 2][:, S * (p // 2) : S * (p // 2 + 1)]
        change = inner_change(
            u, v, m, xp[:, :S], xp[:, S : 2 * S], yp[:16], yp[16:32], xp[:, 2 * S :] + yp[32:]
        )
        z = second_difference(lambda i: values[i], p)
        sections.append(values[p] + (wet_of(levels, k) * change + lift_of(levels, k) * z))
    pack_rims(tile, x_rim, lambda p: sections[p][:8], lambda p: sections[p][8:], rims_out)


def middle_kernel(
    start,
    flow,
    levels,
    neighbours,
    mate,
    own,
    other,
    right,
    left,
    along,
    right_rim_packed,
    left_rim,
    after,
    out,
    section,
):
    tile = lax.axis_index("tile")
    near = beside(neighbours, tile)
    received = (mate, own, other)
    rows, ends = rim_changes(near, tile, received, flow, along, right_rim_packed, left_rim)

    def inner(p, x, y, z):
        k = p % LEVELS
        u, v, mixing = flow_of(flow, k)
        curve = x[:, 2 * S :] + y[2 * S :]
        change = inner_change(
            u, v, mixing, x[:, :S], x[:, S : 2 * S], y[:S], y[S : 2 * S], curve
        )
        return wet_of(levels, k) * change + lift_of(levels, k) * z

    def first(p, x, y, z):
        plane = start[p] + (inner(p, x, y, z) + rows(p))
        section[p] = add_ends(plane, wet_of(levels, p % LEVELS) * ends(p))

    def second(p, x, y, z):
        out[p] = 0.5 * (start[p] + section[p] + inner(p, x, y, z))

    inner_sums(lambda p: start[p], right, left, first)
    inner_sums(lambda p: section[p], right, left, second)


def last_kernel(
    inner,
    flow,
    levels,
    neighbours,
    mate,
    own,
    other,
    along,
    right_rim_packed,
    left_rim,
    out,
    held,
    sent,
):
    tile = lax.axis_index("tile")
    near = beside(neighbours, tile)
    received = (mate, own, other)
    rows, ends = rim_changes(near, tile, received, flow, along, right_rim_packed, left_rim)
    copies = []
    for p in range(2 * LEVELS):
        plane = inner[p] + 0.5 * rows(p)
        held[p] = add_ends(plane, (0.5 * wet_of(levels, p % LEVELS)) * ends(p))
        copies.append(pltpu.make_async_copy(held.at[p], out.at[p], sent.at[p]))
        copies[-1].start()
    for copy in copies:
        copy.wait()


VMEM = pl.BlockSpec(memory_space=pltpu.VMEM)
SMEM = pl.BlockSpec(memory_space=pltpu.SMEM)
HBM = pl.BlockSpec(memory_space=pltpu.HBM)
ANY = pl.BlockSpec(memory_space=pl.ANY)
PARAMS = pltpu.CompilerParams(vmem_limit_bytes=24 * 1024 * 1024)
COST = pl.CostEstimate(flops=2 * 10**9, bytes_accessed=8 * 10**6, transcendentals=0)
FIELD = pltpu.VMEM((2 * LEVELS, S, S), jnp.float32)
RIMS = pltpu.VMEM((3, S // 2, S), jnp.bfloat16)


def across(mate, blocks):
    tile = lax.axis_index("tile")
    x_rim = jnp.where(tile % 4 < 2, mate[:1], blocks[:1])
    return lax.ppermute(jnp.concatenate([x_rim, mate[1:2], blocks[2:]], 0), "tile", ACROSS)


def local(
    tracers, east_velocity, north_velocity, diffusivity, vertical_diffusivity, depths, neighbours
):
    planes = 2 * LEVELS
    neighbours = neighbours.T
    inputs = (
        tracers.reshape(planes, S, S),
        east_velocity.reshape(S, S),
        north_velocity.reshape(S, S),
        diffusivity,
        depths,
        neighbours,
        vertical_diffusivity,
    )
    flow, blocks, start, levels = pl.pallas_call(
        first_kernel,
        out_shape=[
            pltpu.HBM((LEVELS, 2 * S + 16, S), jnp.bfloat16),
            RIMS,
            FIELD,
            pltpu.VMEM((2 * LEVELS, S), jnp.float32),
        ],
        in_specs=[HBM] * 3 + [VMEM] + [HBM] * 3,
        out_specs=[HBM] + [VMEM] * 3,
        scratch_shapes=[
            pltpu.VMEM((planes, S, S), jnp.float32),
            pltpu.VMEM((S, S), jnp.bfloat16),
            pltpu.VMEM((S, S), jnp.bfloat16),
            pltpu.SMEM((TILES,), jnp.int32),
            pltpu.SMEM((4, TILES), jnp.int32),
            pltpu.SMEM((LEVELS,), jnp.float32),
            pltpu.VMEM((2 * S + 16, S), jnp.bfloat16),
            pltpu.SemaphoreType.DMA((6,)),
            pltpu.SemaphoreType.DMA((LEVELS,)),
        ],
        compiler_params=PARAMS,
        name="rims",
    )(*(x if x is diffusivity else pltpu.with_memory_space_constraint(x, pltpu.HBM) for x in inputs))
    mate = lax.ppermute(blocks, "tile", MATES)
    flow = lax.all_to_all(flow, "tracer", 0, 0)
    own = across(mate, blocks)
    columns, right, left, right_rim, left_rim, *packed = pl.pallas_call(
        bands_kernel,
        out_shape=[pltpu.VMEM((S, S), jnp.float32)]
        + [
            pltpu.VMEM(shape, jnp.bfloat16)
            for shape in (
                (2 * S, 3 * S),
                (3 * S, 2 * S),
                (S, 3 * S),
                (2, 48, 16),
                (2 * S, 3 * S),
                (S, 3 * S),
                (2, 48, 48),
                (48, 16),
                (S, S),
            )
        ],
        in_specs=[VMEM, SMEM, ANY],
        out_specs=[VMEM] * 10,
        compiler_params=PARAMS,
        cost_estimate=COST,
        name="bands",
    )(start, neighbours, mate)
    own, columns = lax.optimization_barrier((own, columns))
    received = mate, own, lax.ppermute(own, "tile", MATES)
    blocks, along = pl.pallas_call(
        edge_kernel,
        out_shape=[RIMS, pltpu.VMEM((S + 16, S), jnp.float32)],
        in_specs=[VMEM] * 4 + [SMEM] + [VMEM] * 11,
        out_specs=[VMEM] * 2,
        compiler_params=PARAMS,
        name="edges",
    )(start, columns, flow, levels, neighbours, *received, right, right_rim, left, *packed)
    mate = lax.ppermute(blocks, "tile", MATES)
    own = across(mate, blocks)
    inner = pl.pallas_call(
        middle_kernel,
        out_shape=FIELD,
        in_specs=[VMEM] * 3 + [SMEM] + [VMEM] * 8 + [ANY],
        out_specs=VMEM,
        scratch_shapes=[pltpu.VMEM((planes, S, S), jnp.float32)],
        compiler_params=PARAMS,
        cost_estimate=COST,
        name="middle",
    )(start, flow, levels, neighbours, *received, right, left, along, packed[1], left_rim, mate)
    own, inner = lax.optimization_barrier((own, inner))
    received = mate, own, lax.ppermute(own, "tile", MATES)
    out = pl.pallas_call(
        last_kernel,
        out_shape=jax.ShapeDtypeStruct((planes, S, S), jnp.float32),
        in_specs=[VMEM] * 3 + [SMEM] + [VMEM] * 6,
        out_specs=HBM,
        scratch_shapes=[
            pltpu.VMEM((planes, S, S), jnp.float32),
            pltpu.SemaphoreType.DMA((planes,)),
        ],
        compiler_params=PARAMS,
        name="transported",
    )(inner, flow, levels, neighbours, *received, along, packed[1], left_rim)
    return out.reshape(tracers.shape)


def solution(mesh):
    return jax.shard_map(
        local,
        mesh=mesh,
        in_specs=(
            P("tracer", "tile", None, None, None),
            P("tile", "tracer", None, None),
            P("tile", "tracer", None, None),
            P("tile", "tracer"),
            P(),
            P(),
            P(),
        ),
        out_specs=P("tracer", "tile", None, None, None),
        check_vma=False,
    )
```

time: 37.3 us -> 36.5 us (0.979)
  waiting for transfers between devices: 8.23 us -> 5.85 us
  Pallas kernels: 8.31 us -> 9.92 us
    ppermute x2, waiting for transfers between devices: 3.82 us -> 1.45 us  [across(): lax.ppermute(jnp.concatenate([x_rim, mate[1:2], blocks[2:]], 0), 'tile',...]
    pallas_call x3 -> x4, Pallas kernels: 6.24 us -> 7.8 us  [the longest x1 3.52 us: local(): pl.pallas_call(middle_kernel, out_shape=FIELD, in_specs=[VMEM] * 3 + [SME...]
  transfers between devices with their start and end apart: 7 -> 7, of which waited for: 6 -> 5; matrix products, arithmetic and copies ran while one was open for 0% -> 0% of each run, Pallas kernels for 4% -> 13%
where the time goes in v3:
time: 36.5 us; the launch traced here: 36.3 us
  starting transfers between devices  19.7 us (54%)
  Pallas kernels  9.92 us (27%)
  waiting for transfers between devices  5.85 us (16%)
  between operations  0.75 us (2%)
    ppermute x2, starting transfers between devices, across(): lax.ppermute(jnp.concatenate([x_rim, mate[1:2], blocks[2:]], 0), 'tile',...  12.4 us
    all_to_all x1, starting transfers between devices, local(): flow = lax.all_to_all(flow, 'tracer', 0, 0)  5.72 us
    pallas_call x1, Pallas kernels, local(): pl.pallas_call(middle_kernel, out_shape=FIELD, in_specs=[VMEM] * 3 + [SME...  3.52 us
    ppermute x2, waiting for transfers between devices, local(): received = (mate, own, lax.ppermute(own, 'tile', MATES))  2.45 us
    pallas_call x1, Pallas kernels, local(): pl.pallas_call(last_kernel, out_shape=jax.ShapeDtypeStruct((planes, S, S)...  2.12 us
    ppermute x2, waiting for transfers between devices, local(): mate = lax.ppermute(blocks, 'tile', MATES)  1.95 us
    pallas_call x1, Pallas kernels, local(): pl.pallas_call(first_kernel, out_shape=[pltpu.HBM((LEVELS, 2 * S + 16, S)...  1.72 us
    ppermute x2, starting transfers between devices, local(): mate = lax.ppermute(blocks, 'tile', MATES)  1.48 us
  transfers between devices with their start and end apart: 7, of which 5 were waited for; matrix products, arithmetic and copies ran while one was open for 0% of the time, Pallas kernels for 13%

profile of v3, /device:TPU:15, one launch (start us, length us, event | category | flops | bytes accessed | tf_op | source)
XLA Modules:
  0.0 36.3 jit_solution(7642208914158713647)
XLA Ops:
  0.7 1.7 %rims.1 = (bf16[8,272,128]{2,1,0:T(8,128)(2,1)}, bf16[3,64,128]{2,1,0:T(8,128)(2,1)S(1)}, f32[16,128,128]{2,1,0:T(8,128)S(1)}, f32[16,128]{1,0:T(8,128)S(1)}) custom-call(f32[16,128,128]{2,1,0:T(8,128)} %bitcast.12, bf16[128,128]{1,0:T(8,128)(2,1)} %bitcast.13, bf16[128,128]{1,0:T(8,128)(2,1)} %bitcast.14, bf16[1,1]{1,0:T(2,128)(2,1)S(6)} %copy.9.mixing, ...), custom_call_target="tpu_custom_call" | custom-call | tf_op jit(solution)/shard_map/rims/pallas_call | solution.py:517
  2.4 5.7 %all-to-all-start = ((bf16[8,272,128]{2,1,0:T(8,128)(2,1)}), bf16[8,272,128]{2,1,0:T(8,128)(2,1)S(1)}, u32[]{:S(2)}, u32[]{:S(2)}) async-start(bf16[8,272,128]{2,1,0:T(8,128)(2,1)} %get-tuple-element.29), calls=%async_computation | async-start | bytes 1114112 | tf_op jit(solution)/shard_map/all_to_all | solution.py:542
  8.1 1.2 %collective-permute-start = (bf16[3,64,128]{2,1,0:T(8,128)(2,1)S(1)}, bf16[3,64,128]{2,1,0:T(8,128)(2,1)S(1)}, u32[]{:S(2)}, u32[]{:S(2)}) collective-permute-start(bf16[3,64,128]{2,1,0:T(8,128)(2,1)S(1)} %get-tuple-element.26), channel_id=1, source_target_pairs={{0,8},{8,0},{16,24},{24,16},{32,40},{40,32},{48,56},{56,48},{64,72... | collective-permute-start | bytes 147464 | tf_op jit(solution)/shard_map/ppermute | solution.py:541
  9.3 0.9 %collective-permute-done.after.mate = bf16[3,64,128]{2,1,0:T(8,128)(2,1)S(1)} collective-permute-done((bf16[3,64,128]{2,1,0:T(8,128)(2,1)S(1)}, bf16[3,64,128]{2,1,0:T(8,128)(2,1)S(1)}, u32[]{:S(2)}, u32[]{:S(2)}) %collective-permute-start) | collective-permute-done | bytes 49184 | tf_op jit(solution)/shard_map/ppermute | solution.py:541
  10.2 0.0 copy-start
  10.3 7.3 %collective-permute-start.1 = (bf16[3,64,128]{2,1,0:T(8,128)(2,1)S(1)}, bf16[3,64,128]{2,1,0:T(8,128)(2,1)S(1)}, u32[]{:S(2)}, u32[]{:S(2)}) collective-permute-start(bf16[3,64,128]{2,1,0:T(8,128)(2,1)S(1)} %pad_maximum_fusion), channel_id=1, source_target_pairs={{0,16},{24,40},{32,48},{56,72},{64,80},{88,104},{96,112},{120,136}... | collective-permute-start | bytes 147464 | tf_op jit(solution)/shard_map/ppermute | solution.py:500
  17.6 0.0 copy-done
  17.6 1.2 %bands.1 = (f32[128,128]{1,0:T(8,128)S(1)}, bf16[256,384]{1,0:T(8,128)(2,1)S(1)}, bf16[384,256]{1,0:T(8,128)(2,1)S(1)}, bf16[128,384]{1,0:T(8,128)(2,1)S(1)}, bf...) custom-call(f32[16,128,128]{2,1,0:T(8,128)S(1)} %get-tuple-element.2, ...), custom_call_target="tpu_custom_call" | custom-call | flops 2000000000 | bytes 8000000 | tf_op jit(solution)/shard_map/bands/pallas_call | solution.py:544
  18.8 1.4 %collective-permute-done.1.own = bf16[3,64,128]{2,1,0:T(8,128)(2,1)S(1)} collective-permute-done((bf16[3,64,128]{2,1,0:T(8,128)(2,1)S(1)}, bf16[3,64,128]{2,1,0:T(8,128)(2,1)S(1)}, u32[]{:S(2)}, u32[]{:S(2)}) %collective-permute-start.1) | collective-permute-done | bytes 49184 | tf_op jit(solution)/shard_map/ppermute | solution.py:500
  20.3 0.0 collective-permute-start.2
  20.3 1.2 %collective-permute-done.2.other = bf16[3,64,128]{2,1,0:T(8,128)(2,1)S(1)} collective-permute-done((bf16[3,64,128]{2,1,0:T(8,128)(2,1)S(1)}, bf16[3,64,128]{2,1,0:T(8,128)(2,1)S(1)}, u32[]{:S(2)}, u32[]{:S(2)}) %collective-permute-start.2) | collective-permute-done | bytes 49184 | tf_op jit(solution)/shard_map/ppermute | solution.py:568
  21.5 0.0 all-to-all-done.flow
  21.5 1.3 %edges.1 = (bf16[3,64,128]{2,1,0:T(8,128)(2,1)S(1)}, f32[144,128]{1,0:T(8,128)S(1)}) custom-call(f32[16,128,128]{2,1,0:T(8,128)S(1)} %get-tuple-element.25.start, f32[128,128]{1,0:T(8,128)S(1)} %get-tuple-element.28.columns, bf16[8,272,128]{2,1,0:T(8,128)(2,1)S(1)} %all-to-all-done.flow, f32[16,128]{1,0:T(8,128)S(1)} %get-tuple-element.30.levels, ...), custom_call_target="tpu_custom_call" | custom-call | tf_op jit(solution)/shard_map/edges/pallas_call | solution.py:569
  22.8 0.2 collective-permute-start.3
  23.1 1.1 %collective-permute-done.3.after.mate = bf16[3,64,128]{2,1,0:T(8,128)(2,1)S(1)} collective-permute-done((bf16[3,64,128]{2,1,0:T(8,128)(2,1)S(1)}, bf16[3,64,128]{2,1,0:T(8,128)(2,1)S(1)}, u32[]{:S(2)}, u32[]{:S(2)}) %collective-permute-start.3) | collective-permute-done | bytes 49184 | tf_op jit(solution)/shard_map/ppermute | solution.py:577
  24.2 5.2 %collective-permute-start.4 = (bf16[3,64,128]{2,1,0:T(8,128)(2,1)S(1)}, bf16[3,64,128]{2,1,0:T(8,128)(2,1)S(1)}, u32[]{:S(2)}, u32[]{:S(2)}) collective-permute-start(bf16[3,64,128]{2,1,0:T(8,128)(2,1)S(1)} %pad_maximum_fusion.1), channel_id=1, source_target_pairs={{0,16},{24,40},{32,48},{56,72},{64,80},{88,104},{96,112},{120,136}... | collective-permute-start | bytes 147464 | tf_op jit(solution)/shard_map/ppermute | solution.py:500
  29.3 3.5 %middle.1.inner = f32[16,128,128]{2,1,0:T(8,128)S(1)} custom-call(f32[16,128,128]{2,1,0:T(8,128)S(1)} %get-tuple-element.25.start, bf16[8,272,128]{2,1,0:T(8,128)(2,1)S(1)} %all-to-all-done.flow, f32[16,128]{1,0:T(8,128)S(1)} %get-tuple-element.30.levels, s32[4,32]{1,0:T(4,128)S(1)} %bitcast.10, bf16[3,64,128]{2,1,0:T(8,128)(2,1)S(1)} %collective-permute-done.after.mate, ...), custom_call_target="tpu_custom_call" | custom-call | flops 2000000000 | bytes 8000000 | tf_op jit(solution)/shard_map/middle/pallas_call | solution.py:579
  32.8 0.0 collective-permute-done.4.own
  32.9 0.1 collective-permute-start.5
  33.0 1.2 %collective-permute-done.5.other = bf16[3,64,128]{2,1,0:T(8,128)(2,1)S(1)} collective-permute-done((bf16[3,64,128]{2,1,0:T(8,128)(2,1)S(1)}, bf16[3,64,128]{2,1,0:T(8,128)(2,1)S(1)}, u32[]{:S(2)}, u32[]{:S(2)}) %collective-permute-start.5) | collective-permute-done | bytes 49184 | tf_op jit(solution)/shard_map/ppermute | solution.py:590
  34.2 2.1 %transported.1 = f32[16,128,128]{2,1,0:T(8,128)} custom-call(f32[16,128,128]{2,1,0:T(8,128)S(1)} %middle.1.inner, bf16[8,272,128]{2,1,0:T(8,128)(2,1)S(1)} %all-to-all-done.flow, f32[16,128]{1,0:T(8,128)S(1)} %get-tuple-element.30.levels, s32[4,32]{1,0:T(4,128)S(1)} %bitcast.11, bf16[3,64,128]{2,1,0:T(8,128)(2,1)S(1)} %collective-permute-done.3.after.mate, ...), custom_call_target="tpu_custom_call" | custom-call | tf_op jit(solution)/shard_map/transported/pallas_call | solution.py:591
  (4 shorter events, 0.0 us)
Async XLA Ops:
  2.4 19.1 %all-to-all-start = ((bf16[8,272,128]{2,1,0:T(8,128)(2,1)}), bf16[8,272,128]{2,1,0:T(8,128)(2,1)S(1)}, u32[]{:S(2)}, u32[]{:S(2)}) async-start(bf16[8,272,128]{2,1,0:T(8,128)(2,1)} %get-tuple-element.29), calls=%async_computation | async-start | bytes 1114112 | tf_op jit(solution)/shard_map/all_to_all | solution.py:542
  8.1 2.1 %collective-permute-start = (bf16[3,64,128]{2,1,0:T(8,128)(2,1)S(1)}, bf16[3,64,128]{2,1,0:T(8,128)(2,1)S(1)}, u32[]{:S(2)}, u32[]{:S(2)}) collective-permute-start(bf16[3,64,128]{2,1,0:T(8,128)(2,1)S(1)} %get-tuple-element.26), channel_id=1, source_target_pairs={{0,8},{8,0},{16,24},{24,16},{32,40},{40,32},{48,56},{56,48},{64,72... | collective-permute-start | bytes 147464 | tf_op jit(solution)/shard_map/ppermute | solution.py:541
  10.2 7.3 %copy-start = (s32[32,4]{0,1:T(4,128)S(1)}, s32[32,4]{0,1:T(4,128)}, u32[]{:S(2)}) copy-start(s32[32,4]{0,1:T(4,128)} %param.13) | copy-start | bytes 1540
  10.3 10.0 %collective-permute-start.1 = (bf16[3,64,128]{2,1,0:T(8,128)(2,1)S(1)}, bf16[3,64,128]{2,1,0:T(8,128)(2,1)S(1)}, u32[]{:S(2)}, u32[]{:S(2)}) collective-permute-start(bf16[3,64,128]{2,1,0:T(8,128)(2,1)S(1)} %pad_maximum_fusion), channel_id=1, source_target_pairs={{0,16},{24,40},{32,48},{56,72},{64,80},{88,104},{96,112},{120,136}... | collective-permute-start | bytes 147464 | tf_op jit(solution)/shard_map/ppermute | solution.py:500
  20.3 1.2 %collective-permute-start.2 = (bf16[3,64,128]{2,1,0:T(8,128)(2,1)S(1)}, bf16[3,64,128]{2,1,0:T(8,128)(2,1)S(1)}, u32[]{:S(2)}, u32[]{:S(2)}) collective-permute-start(bf16[3,64,128]{2,1,0:T(8,128)(2,1)S(1)} %collective-permute-done.1.own), channel_id=1, source_target_pairs={{0,8},{8,0},{16,24},{24,16},{32,40},{40,32},{48,56},{56,48},{64,72... | collective-permute-start | bytes 147464 | tf_op jit(solution)/shard_map/ppermute | solution.py:568
  22.8 1.3 %collective-permute-start.3 = (bf16[3,64,128]{2,1,0:T(8,128)(2,1)S(1)}, bf16[3,64,128]{2,1,0:T(8,128)(2,1)S(1)}, u32[]{:S(2)}, u32[]{:S(2)}) collective-permute-start(bf16[3,64,128]{2,1,0:T(8,128)(2,1)S(1)} %get-tuple-element.40), channel_id=1, source_target_pairs={{0,8},{8,0},{16,24},{24,16},{32,40},{40,32},{48,56},{56,48},{64,72... | collective-permute-start | bytes 147464 | tf_op jit(solution)/shard_map/ppermute | solution.py:577
  24.2 8.7 %collective-permute-start.4 = (bf16[3,64,128]{2,1,0:T(8,128)(2,1)S(1)}, bf16[3,64,128]{2,1,0:T(8,128)(2,1)S(1)}, u32[]{:S(2)}, u32[]{:S(2)}) collective-permute-start(bf16[3,64,128]{2,1,0:T(8,128)(2,1)S(1)} %pad_maximum_fusion.1), channel_id=1, source_target_pairs={{0,16},{24,40},{32,48},{56,72},{64,80},{88,104},{96,112},{120,136}... | collective-permute-start | bytes 147464 | tf_op jit(solution)/shard_map/ppermute | solution.py:500
  32.9 1.3 %collective-permute-start.5 = (bf16[3,64,128]{2,1,0:T(8,128)(2,1)S(1)}, bf16[3,64,128]{2,1,0:T(8,128)(2,1)S(1)}, u32[]{:S(2)}, u32[]{:S(2)}) collective-permute-start(bf16[3,64,128]{2,1,0:T(8,128)(2,1)S(1)} %collective-permute-done.4.own), channel_id=1, source_target_pairs={{0,8},{8,0},{16,24},{24,16},{32,40},{40,32},{48,56},{56,48},{64,72... | collective-permute-start | bytes 147464 | tf_op jit(solution)/shard_map/ppermute | solution.py:590

commit v4 on v3

--- a/solution.py
+++ b/solution.py
@@ -22,9 +22,8 @@
     return (tile % 4 == 0) | (tile % 4 == 3)
 
 
-def beside(neighbours, tile):
-    row = [neighbours[e, tile] for e in range(4)]
-    return [jnp.where(slot < 0, -9, slot) for slot in row]
+def beside(levels):
+    return [levels[2 * LEVELS + e : 2 * LEVELS + e + 1] for e in range(4)]
 
 
 def band(distance, coefficients):
@@ -123,6 +122,10 @@
         wet = (k < depth).astype(jnp.float32)
         levels_out[k : k + 1] = jnp.full((1, S), wet, jnp.float32)
         levels_out[LEVELS + k : LEVELS + k + 1] = jnp.full((1, S), wet * vertical[k], jnp.float32)
+    for e in range(4):
+        slot = neighbours[e, tile]
+        slot = jnp.where(slot < 0, -9, slot).astype(jnp.float32)
+        levels_out[2 * LEVELS + e : 2 * LEVELS + e + 1] = jnp.full((1, S), slot, jnp.float32)
     for p in range(2 * LEVELS):
         start_out[p] = tracers[p] * (p % LEVELS < depth).astype(jnp.float32)
     rims(start_out, neighbours[1, tile] >= 0, tile, rims_out)
@@ -135,12 +138,12 @@
     mate, own, other = received
     chip = tile // 2
     for steps in (-2, -1, 1, 2):
-        slot = tile + steps
+        slot = (tile + steps).astype(jnp.float32)
         from_chip = (tile + 2 * TILES + steps) // 2 - TILES
         is_mate = from_chip == chip
         is_own = (from_chip > chip) == looks_up(tile)
         pair = jnp.minimum(from_chip, chip)
-        y_at = jnp.where((slot - pair) % 2 == 0, 2, 1)
+        y_at = jnp.where((tile + steps - pair) % 2 == 0, 2, 1)
         if abs(steps) == 1:
             in_row = (slot == near[0]) | (slot == near[1])
             block = jnp.where(is_own, own[0], other[0])
@@ -192,13 +195,12 @@
     change = carried(u, along[S : S + 1], sums[:, :S], sums[:, S : 2 * S], sums[:, 2 * S :])
     packed = along[S + 8 : S + 9] * change
     side_east = near[1] >= 0
-    lane = iota((S, S), 1)
-    window = lane - jnp.where(side_east, S - 8, 0)
-    in_window = (window >= 0) & (window < 8)
-    back = jnp.where(side_east, S - 8, S)
+    packed = jnp.where(side_east, pltpu.roll(packed, S - 8, 1), packed)
+    window = jnp.where(side_east, 15, 0)
+    in_window = iota((S, S), 1) // 8 == window
 
     def rows(p):
-        return jnp.where(in_window, pltpu.roll(packed, back - 8 * p, 1), 0.0)
+        return jnp.where(in_window, pltpu.roll(packed, (S - 8 * p) % S, 1), 0.0)
 
     sums_y = []
     for odd in range(2):
@@ -304,7 +306,6 @@
     columns,
     flow,
     levels,
-    neighbours,
     mate,
     own,
     other,
@@ -320,21 +321,29 @@
     along_out,
 ):
     tile = lax.axis_index("tile")
-    near = beside(neighbours, tile)
+    near = beside(levels)
     gx, gs, gn = ghosts(near, tile, (mate, own, other))
     planes = 2 * LEVELS
 
-    shift = jnp.where(near[1] >= 0, 8, 0)
+    side_east = near[1] >= 0
     block = iota((S, S), 1) // 8
-    u_packed = jnp.zeros((S, S), jnp.float32)
-    v_packed = jnp.zeros((S, S), jnp.float32)
+
+    def gather(arrays):
+        first = last = jnp.zeros(arrays[0].shape, jnp.float32)
+        at = block[: first.shape[0]]
+        for p, array in enumerate(arrays):
+            rolled = pltpu.roll(array, 8 * p, 1) if p else array
+            first = jnp.where(at == p, rolled, first)
+            last = jnp.where(at == (p + 15) % 16, rolled, last)
+        return jnp.where(side_east, pltpu.roll(last, 8, 1), first)
+
+    flows = [flow_of(flow, k) for k in range(LEVELS)]
+    u_packed = gather([u for u, _, _ in flows])
+    v_packed = gather([v for _, v, _ in flows])
     row_block = block[:1] % LEVELS
     mixing, wet, lift = (jnp.zeros((1, S), jnp.float32) for _ in range(3))
     for k in range(LEVELS):
-        u, v, m = flow_of(flow, k)
-        u_packed = jnp.where(block == k, pltpu.roll(u, shift + 8 * k, 1), u_packed)
-        v_packed = jnp.where(block == k, pltpu.roll(v, shift + 8 * k, 1), v_packed)
-        mixing = jnp.where(row_block == k, m, mixing)
+        mixing = jnp.where(row_block == k, flows[k][2], mixing)
         wet = jnp.where(row_block == k, wet_of(levels, k), wet)
         lift = jnp.where(row_block == k, lift_of(levels, k), lift)
     u_packed = jnp.where(block < LEVELS, u_packed, pltpu.roll(u_packed, S // 2, 1))
@@ -343,15 +352,15 @@
     along_out[S : S + 8] = jnp.broadcast_to(mixing, (8, S))
     along_out[S + 8 :] = jnp.broadcast_to(wet, (8, S))
     low = iota((8, S), 0) < 4
-    rim = jnp.zeros((8, S), jnp.float32)
+    both_rims = []
     for p in range(planes):
         at = 8 * (p // 2)
         pair = (gs[at : at + 8], gn[at : at + 8])
         if p % 2:
-            both = jnp.where(low, pltpu.roll(pair[0], 4, 0), pair[1])
+            both_rims.append(jnp.where(low, pltpu.roll(pair[0], 4, 0), pair[1]))
         else:
-            both = jnp.where(low, pair[0], pltpu.roll(pair[1], 4, 0))
-        rim = jnp.where(block[:8] == p, pltpu.roll(both, shift + 8 * p, 1), rim)
+            both_rims.append(jnp.where(low, pair[0], pltpu.roll(pair[1], 4, 0)))
+    rim = gather(both_rims)
     rim = jnp.concatenate([rim, jnp.zeros_like(rim)], 0).astype(jnp.bfloat16)
     q = columns[...]
     parts = split(q)
@@ -417,7 +426,6 @@
     start,
     flow,
     levels,
-    neighbours,
     mate,
     own,
     other,
@@ -431,7 +439,7 @@
     section,
 ):
     tile = lax.axis_index("tile")
-    near = beside(neighbours, tile)
+    near = beside(levels)
     received = (mate, own, other)
     rows, ends = rim_changes(near, tile, received, flow, along, right_rim_packed, left_rim)
 
@@ -459,7 +467,6 @@
     inner,
     flow,
     levels,
-    neighbours,
     mate,
     own,
     other,
@@ -471,7 +478,7 @@
     sent,
 ):
     tile = lax.axis_index("tile")
-    near = beside(neighbours, tile)
+    near = beside(levels)
     received = (mate, own, other)
     rows, ends = rim_changes(near, tile, received, flow, along, right_rim_packed, left_rim)
     copies = []
@@ -520,7 +527,7 @@
             pltpu.HBM((LEVELS, 2 * S + 16, S), jnp.bfloat16),
             RIMS,
             FIELD,
-            pltpu.VMEM((2 * LEVELS, S), jnp.float32),
+            pltpu.VMEM((3 * LEVELS, S), jnp.float32),
         ],
         in_specs=[HBM] * 3 + [VMEM] + [HBM] * 3,
         out_specs=[HBM] + [VMEM] * 3,
@@ -569,29 +576,29 @@
     blocks, along = pl.pallas_call(
         edge_kernel,
         out_shape=[RIMS, pltpu.VMEM((S + 16, S), jnp.float32)],
-        in_specs=[VMEM] * 4 + [SMEM] + [VMEM] * 11,
+        in_specs=[VMEM] * 15,
         out_specs=[VMEM] * 2,
         compiler_params=PARAMS,
         name="edges",
-    )(start, columns, flow, levels, neighbours, *received, right, right_rim, left, *packed)
+    )(start, columns, flow, levels, *received, right, right_rim, left, *packed)
     mate = lax.ppermute(blocks, "tile", MATES)
     own = across(mate, blocks)
     inner = pl.pallas_call(
         middle_kernel,
         out_shape=FIELD,
-        in_specs=[VMEM] * 3 + [SMEM] + [VMEM] * 8 + [ANY],
+        in_specs=[VMEM] * 11 + [ANY],
         out_specs=VMEM,
         scratch_shapes=[pltpu.VMEM((planes, S, S), jnp.float32)],
         compiler_params=PARAMS,
         cost_estimate=COST,
         name="middle",
-    )(start, flow, levels, neighbours, *received, right, left, along, packed[1], left_rim, mate)
+    )(start, flow, levels, *received, right, left, along, packed[1], left_rim, mate)
     own, inner = lax.optimization_barrier((own, inner))
     received = mate, own, lax.ppermute(own, "tile", MATES)
     out = pl.pallas_call(
         last_kernel,
         out_shape=jax.ShapeDtypeStruct((planes, S, S), jnp.float32),
-        in_specs=[VMEM] * 3 + [SMEM] + [VMEM] * 6,
+        in_specs=[VMEM] * 9,
         out_specs=HBM,
         scratch_shapes=[
             pltpu.VMEM((planes, S, S), jnp.float32),
@@ -599,7 +606,7 @@
         ],
         compiler_params=PARAMS,
         name="transported",
-    )(inner, flow, levels, neighbours, *received, along, packed[1], left_rim)
+    )(inner, flow, levels, *received, along, packed[1], left_rim)
     return out.reshape(tracers.shape)
 
 

time: 36.5 us -> 35.1 us (0.962)
  Pallas kernels: 9.92 us -> 8.47 us
    pallas_call x1, Pallas kernels: 3.52 us -> 2.99 us  [local(): pl.pallas_call(middle_kernel, out_shape=FIELD, in_specs=[VMEM] * 11 + [AN...]
    pallas_call x1, Pallas kernels: 2.12 us -> 1.65 us  [local(): pl.pallas_call(last_kernel, out_shape=jax.ShapeDtypeStruct((planes, S, S)...]
    pallas_call x1, Pallas kernels: 1.32 us -> 0.88 us  [local(): pl.pallas_call(edge_kernel, out_shape=[RIMS, pltpu.VMEM((S + 16, S), jnp....]
  transfers between devices with their start and end apart: 7 -> 7, of which waited for: 5 -> 5; matrix products, arithmetic and copies ran while one was open for 0% -> 0% of each run, Pallas kernels for 13% -> 12%
where the time goes in v4:
time: 35.1 us; the launch traced here: 34.8 us
  starting transfers between devices  19.7 us (56%)
  Pallas kernels  8.47 us (24%)
  waiting for transfers between devices  5.85 us (17%)
  between operations  0.75 us (2%)
    ppermute x2, starting transfers between devices, across(): lax.ppermute(jnp.concatenate([x_rim, mate[1:2], blocks[2:]], 0), 'tile',...  12.4 us
    all_to_all x1, starting transfers between devices, local(): flow = lax.all_to_all(flow, 'tracer', 0, 0)  5.72 us
    pallas_call x1, Pallas kernels, local(): pl.pallas_call(middle_kernel, out_shape=FIELD, in_specs=[VMEM] * 11 + [AN...  2.99 us
    ppermute x2, waiting for transfers between devices, local(): received = (mate, own, lax.ppermute(own, 'tile', MATES))  2.45 us
    ppermute x2, waiting for transfers between devices, local(): mate = lax.ppermute(blocks, 'tile', MATES)  1.95 us
    pallas_call x1, Pallas kernels, local(): pl.pallas_call(first_kernel, out_shape=[pltpu.HBM((LEVELS, 2 * S + 16, S)...  1.73 us
    pallas_call x1, Pallas kernels, local(): pl.pallas_call(last_kernel, out_shape=jax.ShapeDtypeStruct((planes, S, S)...  1.65 us
    ppermute x2, starting transfers between devices, local(): mate = lax.ppermute(blocks, 'tile', MATES)  1.48 us
  transfers between devices with their start and end apart: 7, of which 5 were waited for; matrix products, arithmetic and copies ran while one was open for 0% of the time, Pallas kernels for 12%

profile of v4, /device:TPU:15, one launch (start us, length us, event | category | flops | bytes accessed | tf_op | source)
XLA Modules:
  0.0 34.8 jit_solution(10970705568886491072)
XLA Ops:
  0.7 1.7 %rims.1 = (bf16[8,272,128]{2,1,0:T(8,128)(2,1)}, bf16[3,64,128]{2,1,0:T(8,128)(2,1)S(1)}, f32[16,128,128]{2,1,0:T(8,128)S(1)}, f32[24,128]{1,0:T(8,128)S(1)}) custom-call(f32[16,128,128]{2,1,0:T(8,128)} %bitcast.9, bf16[128,128]{1,0:T(8,128)(2,1)} %bitcast.10, bf16[128,128]{1,0:T(8,128)(2,1)} %bitcast.11, bf16[1,1]{1,0:T(2,128)(2,1)S(6)} %copy.9.mixing, ...), custom_call_target="tpu_custom_call" | custom-call | tf_op jit(solution)/shard_map/rims/pallas_call | solution.py:524
  2.4 5.7 %all-to-all-start = ((bf16[8,272,128]{2,1,0:T(8,128)(2,1)}), bf16[8,272,128]{2,1,0:T(8,128)(2,1)S(1)}, u32[]{:S(2)}, u32[]{:S(2)}) async-start(bf16[8,272,128]{2,1,0:T(8,128)(2,1)} %get-tuple-element.29), calls=%async_computation | async-start | bytes 1114112 | tf_op jit(solution)/shard_map/all_to_all | solution.py:549
  8.1 1.2 %collective-permute-start = (bf16[3,64,128]{2,1,0:T(8,128)(2,1)S(1)}, bf16[3,64,128]{2,1,0:T(8,128)(2,1)S(1)}, u32[]{:S(2)}, u32[]{:S(2)}) collective-permute-start(bf16[3,64,128]{2,1,0:T(8,128)(2,1)S(1)} %get-tuple-element.26), channel_id=1, source_target_pairs={{0,8},{8,0},{16,24},{24,16},{32,40},{40,32},{48,56},{56,48},{64,72... | collective-permute-start | bytes 147464 | tf_op jit(solution)/shard_map/ppermute | solution.py:548
  9.4 0.9 %collective-permute-done.after.mate = bf16[3,64,128]{2,1,0:T(8,128)(2,1)S(1)} collective-permute-done((bf16[3,64,128]{2,1,0:T(8,128)(2,1)S(1)}, bf16[3,64,128]{2,1,0:T(8,128)(2,1)S(1)}, u32[]{:S(2)}, u32[]{:S(2)}) %collective-permute-start) | collective-permute-done | bytes 49184 | tf_op jit(solution)/shard_map/ppermute | solution.py:548
  10.2 0.0 copy-start
  10.3 7.3 %collective-permute-start.1 = (bf16[3,64,128]{2,1,0:T(8,128)(2,1)S(1)}, bf16[3,64,128]{2,1,0:T(8,128)(2,1)S(1)}, u32[]{:S(2)}, u32[]{:S(2)}) collective-permute-start(bf16[3,64,128]{2,1,0:T(8,128)(2,1)S(1)} %pad_maximum_fusion), channel_id=1, source_target_pairs={{0,16},{24,40},{32,48},{56,72},{64,80},{88,104},{96,112},{120,136}... | collective-permute-start | bytes 147464 | tf_op jit(solution)/shard_map/ppermute | solution.py:507
  17.6 0.0 copy-done
  17.6 1.2 %bands.1 = (f32[128,128]{1,0:T(8,128)S(1)}, bf16[256,384]{1,0:T(8,128)(2,1)S(1)}, bf16[384,256]{1,0:T(8,128)(2,1)S(1)}, bf16[128,384]{1,0:T(8,128)(2,1)S(1)}, bf...) custom-call(f32[16,128,128]{2,1,0:T(8,128)S(1)} %get-tuple-element.2, ...), custom_call_target="tpu_custom_call" | custom-call | flops 2000000000 | bytes 8000000 | tf_op jit(solution)/shard_map/bands/pallas_call | solution.py:551
  18.8 1.4 %collective-permute-done.1.own = bf16[3,64,128]{2,1,0:T(8,128)(2,1)S(1)} collective-permute-done((bf16[3,64,128]{2,1,0:T(8,128)(2,1)S(1)}, bf16[3,64,128]{2,1,0:T(8,128)(2,1)S(1)}, u32[]{:S(2)}, u32[]{:S(2)}) %collective-permute-start.1) | collective-permute-done | bytes 49184 | tf_op jit(solution)/shard_map/ppermute | solution.py:507
  20.3 0.0 collective-permute-start.2
  20.3 1.2 %collective-permute-done.2.other = bf16[3,64,128]{2,1,0:T(8,128)(2,1)S(1)} collective-permute-done((bf16[3,64,128]{2,1,0:T(8,128)(2,1)S(1)}, bf16[3,64,128]{2,1,0:T(8,128)(2,1)S(1)}, u32[]{:S(2)}, u32[]{:S(2)}) %collective-permute-start.2) | collective-permute-done | bytes 49184 | tf_op jit(solution)/shard_map/ppermute | solution.py:575
  21.5 0.0 all-to-all-done.flow
  21.5 0.9 %edges.1 = (bf16[3,64,128]{2,1,0:T(8,128)(2,1)S(1)}, f32[144,128]{1,0:T(8,128)S(1)}) custom-call(f32[16,128,128]{2,1,0:T(8,128)S(1)} %get-tuple-element.25.start, f32[128,128]{1,0:T(8,128)S(1)} %get-tuple-element.28.columns, bf16[8,272,128]{2,1,0:T(8,128)(2,1)S(1)} %all-to-all-done.flow, f32[24,128]{1,0:T(8,128)S(1)} %get-tuple-element.30.levels, ...), custom_call_target="tpu_custom_call" | custom-call | tf_op jit(solution)/shard_map/edges/pallas_call | solution.py:576
  22.4 0.2 collective-permute-start.3
  22.6 1.1 %collective-permute-done.3.after.mate = bf16[3,64,128]{2,1,0:T(8,128)(2,1)S(1)} collective-permute-done((bf16[3,64,128]{2,1,0:T(8,128)(2,1)S(1)}, bf16[3,64,128]{2,1,0:T(8,128)(2,1)S(1)}, u32[]{:S(2)}, u32[]{:S(2)}) %collective-permute-start.3) | collective-permute-done | bytes 49184 | tf_op jit(solution)/shard_map/ppermute | solution.py:584
  23.7 5.2 %collective-permute-start.4 = (bf16[3,64,128]{2,1,0:T(8,128)(2,1)S(1)}, bf16[3,64,128]{2,1,0:T(8,128)(2,1)S(1)}, u32[]{:S(2)}, u32[]{:S(2)}) collective-permute-start(bf16[3,64,128]{2,1,0:T(8,128)(2,1)S(1)} %pad_maximum_fusion.1), channel_id=1, source_target_pairs={{0,16},{24,40},{32,48},{56,72},{64,80},{88,104},{96,112},{120,136}... | collective-permute-start | bytes 147464 | tf_op jit(solution)/shard_map/ppermute | solution.py:507
  28.9 3.0 %middle.1.inner = f32[16,128,128]{2,1,0:T(8,128)S(1)} custom-call(f32[16,128,128]{2,1,0:T(8,128)S(1)} %get-tuple-element.25.start, bf16[8,272,128]{2,1,0:T(8,128)(2,1)S(1)} %all-to-all-done.flow, f32[24,128]{1,0:T(8,128)S(1)} %get-tuple-element.30.levels, bf16[3,64,128]{2,1,0:T(8,128)(2,1)S(1)} %collective-permute-done.after.mate, ...), custom_call_target="tpu_custom_call" | custom-call | flops 2000000000 | bytes 8000000 | tf_op jit(solution)/shard_map/middle/pallas_call | solution.py:586
  31.9 0.0 collective-permute-done.4.own
  31.9 0.1 collective-permute-start.5
  32.0 1.2 %collective-permute-done.5.other = bf16[3,64,128]{2,1,0:T(8,128)(2,1)S(1)} collective-permute-done((bf16[3,64,128]{2,1,0:T(8,128)(2,1)S(1)}, bf16[3,64,128]{2,1,0:T(8,128)(2,1)S(1)}, u32[]{:S(2)}, u32[]{:S(2)}) %collective-permute-start.5) | collective-permute-done | bytes 49184 | tf_op jit(solution)/shard_map/ppermute | solution.py:597
  33.2 1.6 %transported.1 = f32[16,128,128]{2,1,0:T(8,128)} custom-call(f32[16,128,128]{2,1,0:T(8,128)S(1)} %middle.1.inner, bf16[8,272,128]{2,1,0:T(8,128)(2,1)S(1)} %all-to-all-done.flow, f32[24,128]{1,0:T(8,128)S(1)} %get-tuple-element.30.levels, bf16[3,64,128]{2,1,0:T(8,128)(2,1)S(1)} %collective-permute-done.3.after.mate, ...), custom_call_target="tpu_custom_call" | custom-call | tf_op jit(solution)/shard_map/transported/pallas_call | solution.py:598
  (4 shorter events, 0.0 us)
Async XLA Ops:
  2.4 19.1 %all-to-all-start = ((bf16[8,272,128]{2,1,0:T(8,128)(2,1)}), bf16[8,272,128]{2,1,0:T(8,128)(2,1)S(1)}, u32[]{:S(2)}, u32[]{:S(2)}) async-start(bf16[8,272,128]{2,1,0:T(8,128)(2,1)} %get-tuple-element.29), calls=%async_computation | async-start | bytes 1114112 | tf_op jit(solution)/shard_map/all_to_all | solution.py:549
  8.1 2.1 %collective-permute-start = (bf16[3,64,128]{2,1,0:T(8,128)(2,1)S(1)}, bf16[3,64,128]{2,1,0:T(8,128)(2,1)S(1)}, u32[]{:S(2)}, u32[]{:S(2)}) collective-permute-start(bf16[3,64,128]{2,1,0:T(8,128)(2,1)S(1)} %get-tuple-element.26), channel_id=1, source_target_pairs={{0,8},{8,0},{16,24},{24,16},{32,40},{40,32},{48,56},{56,48},{64,72... | collective-permute-start | bytes 147464 | tf_op jit(solution)/shard_map/ppermute | solution.py:548
  10.2 7.3 %copy-start = (s32[32,4]{0,1:T(4,128)S(1)}, s32[32,4]{0,1:T(4,128)}, u32[]{:S(2)}) copy-start(s32[32,4]{0,1:T(4,128)} %param.13) | copy-start | bytes 1540
  10.3 10.0 %collective-permute-start.1 = (bf16[3,64,128]{2,1,0:T(8,128)(2,1)S(1)}, bf16[3,64,128]{2,1,0:T(8,128)(2,1)S(1)}, u32[]{:S(2)}, u32[]{:S(2)}) collective-permute-start(bf16[3,64,128]{2,1,0:T(8,128)(2,1)S(1)} %pad_maximum_fusion), channel_id=1, source_target_pairs={{0,16},{24,40},{32,48},{56,72},{64,80},{88,104},{96,112},{120,136}... | collective-permute-start | bytes 147464 | tf_op jit(solution)/shard_map/ppermute | solution.py:507
  20.3 1.2 %collective-permute-start.2 = (bf16[3,64,128]{2,1,0:T(8,128)(2,1)S(1)}, bf16[3,64,128]{2,1,0:T(8,128)(2,1)S(1)}, u32[]{:S(2)}, u32[]{:S(2)}) collective-permute-start(bf16[3,64,128]{2,1,0:T(8,128)(2,1)S(1)} %collective-permute-done.1.own), channel_id=1, source_target_pairs={{0,8},{8,0},{16,24},{24,16},{32,40},{40,32},{48,56},{56,48},{64,72... | collective-permute-start | bytes 147464 | tf_op jit(solution)/shard_map/ppermute | solution.py:575
  22.4 1.3 %collective-permute-start.3 = (bf16[3,64,128]{2,1,0:T(8,128)(2,1)S(1)}, bf16[3,64,128]{2,1,0:T(8,128)(2,1)S(1)}, u32[]{:S(2)}, u32[]{:S(2)}) collective-permute-start(bf16[3,64,128]{2,1,0:T(8,128)(2,1)S(1)} %get-tuple-element.40), channel_id=1, source_target_pairs={{0,8},{8,0},{16,24},{24,16},{32,40},{40,32},{48,56},{56,48},{64,72... | collective-permute-start | bytes 147464 | tf_op jit(solution)/shard_map/ppermute | solution.py:584
  23.7 8.2 %collective-permute-start.4 = (bf16[3,64,128]{2,1,0:T(8,128)(2,1)S(1)}, bf16[3,64,128]{2,1,0:T(8,128)(2,1)S(1)}, u32[]{:S(2)}, u32[]{:S(2)}) collective-permute-start(bf16[3,64,128]{2,1,0:T(8,128)(2,1)S(1)} %pad_maximum_fusion.1), channel_id=1, source_target_pairs={{0,16},{24,40},{32,48},{56,72},{64,80},{88,104},{96,112},{120,136}... | collective-permute-start | bytes 147464 | tf_op jit(solution)/shard_map/ppermute | solution.py:507
  31.9 1.3 %collective-permute-start.5 = (bf16[3,64,128]{2,1,0:T(8,128)(2,1)S(1)}, bf16[3,64,128]{2,1,0:T(8,128)(2,1)S(1)}, u32[]{:S(2)}, u32[]{:S(2)}) collective-permute-start(bf16[3,64,128]{2,1,0:T(8,128)(2,1)S(1)} %collective-permute-done.4.own), channel_id=1, source_target_pairs={{0,8},{8,0},{16,24},{24,16},{32,40},{40,32},{48,56},{56,48},{64,72... | collective-permute-start | bytes 147464 | tf_op jit(solution)/shard_map/ppermute | solution.py:597

commit v5 on v4

--- a/solution.py
+++ b/solution.py
@@ -8,6 +8,7 @@
 S = 128
 LEVELS = 8
 TILES = 32
+PIECES = 4
 AHEAD = (-2.0, 15.0, -60.0, 20.0, 30.0, -3.0, 0.0)
 BEHIND = (0.0, 3.0, -30.0, -20.0, 60.0, -15.0, 2.0)
 CURVE = (0.0, 0.0, 1.0, -2.0, 1.0, 0.0, 0.0)
@@ -56,15 +57,6 @@
     out[0] = x_rim.astype(jnp.bfloat16)
     out[1] = jnp.where(up, south, north).astype(jnp.bfloat16)
     out[2] = jnp.where(up, north, south).astype(jnp.bfloat16)
-
-
-def rims(field, side_east, tile, out):
-    lane = iota((S, S), 1)
-    shift = jnp.where(side_east, 4, 0)
-    x_rim = jnp.zeros((S, S), jnp.float32)
-    for p in range(2 * LEVELS):
-        x_rim = jnp.where(lane // 4 == p, pltpu.roll(field[p], shift + 4 * p, 1), x_rim)
-    pack_rims(tile, x_rim, lambda p: field[p, :8], lambda p: field[p, S - 8 :], out)
 
 
 def first_kernel(
@@ -89,8 +81,14 @@
     arrived,
     sent,
 ):
-    copies = [
-        pltpu.make_async_copy(source, target, arrived.at[i])
+    planes = 2 * LEVELS
+    piece = planes // PIECES
+    pieces = [
+        pltpu.make_async_copy(tracers_in.at[at], tracers.at[at], arrived.at[i])
+        for i, at in enumerate(pl.ds(i * piece, piece) for i in range(PIECES))
+    ]
+    small = [
+        pltpu.make_async_copy(source, target, arrived.at[PIECES + i])
         for i, (source, target) in enumerate(
             (
                 (east_in, east),
@@ -98,13 +96,12 @@
                 (depths_in, depths),
                 (neighbours_in, neighbours),
                 (vertical_in, vertical),
-                (tracers_in, tracers),
             )
         )
     ]
-    for copy in copies:
+    for copy in small[:2] + pieces + small[2:]:
         copy.start()
-    for copy in copies[:2]:
+    for copy in small[:2]:
         copy.wait()
     block[:S] = east[...]
     block[S : 2 * S] = north[...]
@@ -113,7 +110,7 @@
     leaving = [pltpu.make_async_copy(block, flow_out.at[j], sent.at[j]) for j in range(LEVELS)]
     for copy in leaving:
         copy.start()
-    for copy in copies[2:]:
+    for copy in small[2:]:
         copy.wait()
     tile = lax.axis_index("tile")
     depth = depths[tile]
@@ -126,9 +123,18 @@
         slot = neighbours[e, tile]
         slot = jnp.where(slot < 0, -9, slot).astype(jnp.float32)
         levels_out[2 * LEVELS + e : 2 * LEVELS + e + 1] = jnp.full((1, S), slot, jnp.float32)
-    for p in range(2 * LEVELS):
-        start_out[p] = tracers[p] * (p % LEVELS < depth).astype(jnp.float32)
-    rims(start_out, neighbours[1, tile] >= 0, tile, rims_out)
+    lane = iota((S, S), 1)
+    shift = jnp.where(neighbours[1, tile] >= 0, 4, 0)
+    x_rim = jnp.zeros((S, S), jnp.float32)
+    for p in range(planes):
+        if p % piece == 0:
+            pieces[p // piece].wait()
+        plane = tracers[p] * (p % LEVELS < depth).astype(jnp.float32)
+        start_out[p] = plane
+        x_rim = jnp.where(lane // 4 == p, pltpu.roll(plane, shift + 4 * p, 1), x_rim)
+    pack_rims(
+        tile, x_rim, lambda p: start_out[p, :8], lambda p: start_out[p, S - 8 :], rims_out
+    )
     for copy in leaving:
         copy.wait()
 
@@ -188,12 +194,12 @@
     return z
 
 
-def rim_changes(near, tile, received, flow, along, right_rim_packed, left_rim):
+def rim_changes(near, tile, received, flow, along, right_rim_packed, left_rim, scale=1.0):
     gx, gs, gn = ghosts(near, tile, received)
     sums = dot(gx.astype(jnp.bfloat16), right_rim_packed[...])
     u = along[:S]
     change = carried(u, along[S : S + 1], sums[:, :S], sums[:, S : 2 * S], sums[:, 2 * S :])
-    packed = along[S + 8 : S + 9] * change
+    packed = (scale * along[S + 8 : S + 9]) * change
     side_east = near[1] >= 0
     packed = jnp.where(side_east, pltpu.roll(packed, S - 8, 1), packed)
     window = jnp.where(side_east, 15, 0)
@@ -480,13 +486,15 @@
     tile = lax.axis_index("tile")
     near = beside(levels)
     received = (mate, own, other)
-    rows, ends = rim_changes(near, tile, received, flow, along, right_rim_packed, left_rim)
+    rows, ends = rim_changes(near, tile, received, flow, along, right_rim_packed, left_rim, 0.5)
     copies = []
     for p in range(2 * LEVELS):
-        plane = inner[p] + 0.5 * rows(p)
+        plane = inner[p] + rows(p)
         held[p] = add_ends(plane, (0.5 * wet_of(levels, p % LEVELS)) * ends(p))
-        copies.append(pltpu.make_async_copy(held.at[p], out.at[p], sent.at[p]))
-        copies[-1].start()
+        if p % 2:
+            at = pl.ds(p - 1, 2)
+            copies.append(pltpu.make_async_copy(held.at[at], out.at[at], sent.at[p]))
+            copies[-1].start()
     for copy in copies:
         copy.wait()
 
@@ -539,7 +547,7 @@
             pltpu.SMEM((4, TILES), jnp.int32),
             pltpu.SMEM((LEVELS,), jnp.float32),
             pltpu.VMEM((2 * S + 16, S), jnp.bfloat16),
-            pltpu.SemaphoreType.DMA((6,)),
+            pltpu.SemaphoreType.DMA((PIECES + 5,)),
             pltpu.SemaphoreType.DMA((LEVELS,)),
         ],
         compiler_params=PARAMS,

time: 35.1 us -> 35.2 us (level)
  no operation moved by 1% of the time
where the time goes in v5:
time: 35.2 us; the launch traced here: 34.9 us
  starting transfers between devices  19.7 us (56%)
  Pallas kernels  8.52 us (24%)
  waiting for transfers between devices  5.85 us (17%)
  between operations  0.75 us (2%)
    ppermute x2, starting transfers between devices, across(): lax.ppermute(jnp.concatenate([x_rim, mate[1:2], blocks[2:]], 0), 'tile',...  12.4 us
    all_to_all x1, starting transfers between devices, local(): flow = lax.all_to_all(flow, 'tracer', 0, 0)  5.72 us
    pallas_call x1, Pallas kernels, local(): pl.pallas_call(middle_kernel, out_shape=FIELD, in_specs=[VMEM] * 11 + [AN...  2.98 us
    ppermute x2, waiting for transfers between devices, local(): received = (mate, own, lax.ppermute(own, 'tile', MATES))  2.45 us
    ppermute x2, waiting for transfers between devices, local(): mate = lax.ppermute(blocks, 'tile', MATES)  1.95 us
    pallas_call x1, Pallas kernels, local(): pl.pallas_call(first_kernel, out_shape=[pltpu.HBM((LEVELS, 2 * S + 16, S)...  1.75 us
    pallas_call x1, Pallas kernels, local(): pl.pallas_call(last_kernel, out_shape=jax.ShapeDtypeStruct((planes, S, S)...  1.68 us
    ppermute x2, starting transfers between devices, local(): mate = lax.ppermute(blocks, 'tile', MATES)  1.48 us
  transfers between devices with their start and end apart: 7, of which 5 were waited for; matrix products, arithmetic and copies ran while one was open for 0% of the time, Pallas kernels for 12%

profile of v5, /device:TPU:15, one launch (start us, length us, event | category | flops | bytes accessed | tf_op | source)
XLA Modules:
  0.0 34.9 jit_solution(15956229119288231055)
XLA Ops:
  0.7 1.8 %rims.1 = (bf16[8,272,128]{2,1,0:T(8,128)(2,1)}, bf16[3,64,128]{2,1,0:T(8,128)(2,1)S(1)}, f32[16,128,128]{2,1,0:T(8,128)S(1)}, f32[24,128]{1,0:T(8,128)S(1)}) custom-call(f32[16,128,128]{2,1,0:T(8,128)} %bitcast.9, bf16[128,128]{1,0:T(8,128)(2,1)} %bitcast.10, bf16[128,128]{1,0:T(8,128)(2,1)} %bitcast.11, bf16[1,1]{1,0:T(2,128)(2,1)S(6)} %copy.9.mixing, ...), custom_call_target="tpu_custom_call" | custom-call | tf_op jit(solution)/shard_map/rims/pallas_call | solution.py:532
  2.4 5.7 %all-to-all-start = ((bf16[8,272,128]{2,1,0:T(8,128)(2,1)}), bf16[8,272,128]{2,1,0:T(8,128)(2,1)S(1)}, u32[]{:S(2)}, u32[]{:S(2)}) async-start(bf16[8,272,128]{2,1,0:T(8,128)(2,1)} %get-tuple-element.29), calls=%async_computation | async-start | bytes 1114112 | tf_op jit(solution)/shard_map/all_to_all | solution.py:557
  8.1 1.2 %collective-permute-start = (bf16[3,64,128]{2,1,0:T(8,128)(2,1)S(1)}, bf16[3,64,128]{2,1,0:T(8,128)(2,1)S(1)}, u32[]{:S(2)}, u32[]{:S(2)}) collective-permute-start(bf16[3,64,128]{2,1,0:T(8,128)(2,1)S(1)} %get-tuple-element.26), channel_id=1, source_target_pairs={{0,8},{8,0},{16,24},{24,16},{32,40},{40,32},{48,56},{56,48},{64,72... | collective-permute-start | bytes 147464 | tf_op jit(solution)/shard_map/ppermute | solution.py:556
  9.4 0.9 %collective-permute-done.after.mate = bf16[3,64,128]{2,1,0:T(8,128)(2,1)S(1)} collective-permute-done((bf16[3,64,128]{2,1,0:T(8,128)(2,1)S(1)}, bf16[3,64,128]{2,1,0:T(8,128)(2,1)S(1)}, u32[]{:S(2)}, u32[]{:S(2)}) %collective-permute-start) | collective-permute-done | bytes 49184 | tf_op jit(solution)/shard_map/ppermute | solution.py:556
  10.3 0.0 copy-start
  10.3 7.3 %collective-permute-start.1 = (bf16[3,64,128]{2,1,0:T(8,128)(2,1)S(1)}, bf16[3,64,128]{2,1,0:T(8,128)(2,1)S(1)}, u32[]{:S(2)}, u32[]{:S(2)}) collective-permute-start(bf16[3,64,128]{2,1,0:T(8,128)(2,1)S(1)} %pad_maximum_fusion), channel_id=1, source_target_pairs={{0,16},{24,40},{32,48},{56,72},{64,80},{88,104},{96,112},{120,136}... | collective-permute-start | bytes 147464 | tf_op jit(solution)/shard_map/ppermute | solution.py:515
  17.6 0.0 copy-done
  17.6 1.2 %bands.1 = (f32[128,128]{1,0:T(8,128)S(1)}, bf16[256,384]{1,0:T(8,128)(2,1)S(1)}, bf16[384,256]{1,0:T(8,128)(2,1)S(1)}, bf16[128,384]{1,0:T(8,128)(2,1)S(1)}, bf...) custom-call(f32[16,128,128]{2,1,0:T(8,128)S(1)} %get-tuple-element.2, ...), custom_call_target="tpu_custom_call" | custom-call | flops 2000000000 | bytes 8000000 | tf_op jit(solution)/shard_map/bands/pallas_call | solution.py:559
  18.8 1.4 %collective-permute-done.1.own = bf16[3,64,128]{2,1,0:T(8,128)(2,1)S(1)} collective-permute-done((bf16[3,64,128]{2,1,0:T(8,128)(2,1)S(1)}, bf16[3,64,128]{2,1,0:T(8,128)(2,1)S(1)}, u32[]{:S(2)}, u32[]{:S(2)}) %collective-permute-start.1) | collective-permute-done | bytes 49184 | tf_op jit(solution)/shard_map/ppermute | solution.py:515
  20.3 0.0 collective-permute-start.2
  20.3 1.2 %collective-permute-done.2.other = bf16[3,64,128]{2,1,0:T(8,128)(2,1)S(1)} collective-permute-done((bf16[3,64,128]{2,1,0:T(8,128)(2,1)S(1)}, bf16[3,64,128]{2,1,0:T(8,128)(2,1)S(1)}, u32[]{:S(2)}, u32[]{:S(2)}) %collective-permute-start.2) | collective-permute-done | bytes 49184 | tf_op jit(solution)/shard_map/ppermute | solution.py:583
  21.5 0.0 all-to-all-done.flow
  21.5 0.9 %edges.1 = (bf16[3,64,128]{2,1,0:T(8,128)(2,1)S(1)}, f32[144,128]{1,0:T(8,128)S(1)}) custom-call(f32[16,128,128]{2,1,0:T(8,128)S(1)} %get-tuple-element.25.start, f32[128,128]{1,0:T(8,128)S(1)} %get-tuple-element.28.columns, bf16[8,272,128]{2,1,0:T(8,128)(2,1)S(1)} %all-to-all-done.flow, f32[24,128]{1,0:T(8,128)S(1)} %get-tuple-element.30.levels, ...), custom_call_target="tpu_custom_call" | custom-call | tf_op jit(solution)/shard_map/edges/pallas_call | solution.py:584
  22.4 0.2 collective-permute-start.3
  22.6 1.1 %collective-permute-done.3.after.mate = bf16[3,64,128]{2,1,0:T(8,128)(2,1)S(1)} collective-permute-done((bf16[3,64,128]{2,1,0:T(8,128)(2,1)S(1)}, bf16[3,64,128]{2,1,0:T(8,128)(2,1)S(1)}, u32[]{:S(2)}, u32[]{:S(2)}) %collective-permute-start.3) | collective-permute-done | bytes 49184 | tf_op jit(solution)/shard_map/ppermute | solution.py:592
  23.7 5.2 %collective-permute-start.4 = (bf16[3,64,128]{2,1,0:T(8,128)(2,1)S(1)}, bf16[3,64,128]{2,1,0:T(8,128)(2,1)S(1)}, u32[]{:S(2)}, u32[]{:S(2)}) collective-permute-start(bf16[3,64,128]{2,1,0:T(8,128)(2,1)S(1)} %pad_maximum_fusion.1), channel_id=1, source_target_pairs={{0,16},{24,40},{32,48},{56,72},{64,80},{88,104},{96,112},{120,136}... | collective-permute-start | bytes 147464 | tf_op jit(solution)/shard_map/ppermute | solution.py:515
  28.9 3.0 %middle.1.inner = f32[16,128,128]{2,1,0:T(8,128)S(1)} custom-call(f32[16,128,128]{2,1,0:T(8,128)S(1)} %get-tuple-element.25.start, bf16[8,272,128]{2,1,0:T(8,128)(2,1)S(1)} %all-to-all-done.flow, f32[24,128]{1,0:T(8,128)S(1)} %get-tuple-element.30.levels, bf16[3,64,128]{2,1,0:T(8,128)(2,1)S(1)} %collective-permute-done.after.mate, ...), custom_call_target="tpu_custom_call" | custom-call | flops 2000000000 | bytes 8000000 | tf_op jit(solution)/shard_map/middle/pallas_call | solution.py:594
  31.9 0.0 collective-permute-done.4.own
  31.9 0.1 collective-permute-start.5
  32.0 1.2 %collective-permute-done.5.other = bf16[3,64,128]{2,1,0:T(8,128)(2,1)S(1)} collective-permute-done((bf16[3,64,128]{2,1,0:T(8,128)(2,1)S(1)}, bf16[3,64,128]{2,1,0:T(8,128)(2,1)S(1)}, u32[]{:S(2)}, u32[]{:S(2)}) %collective-permute-start.5) | collective-permute-done | bytes 49184 | tf_op jit(solution)/shard_map/ppermute | solution.py:605
  33.2 1.7 %transported.1 = f32[16,128,128]{2,1,0:T(8,128)} custom-call(f32[16,128,128]{2,1,0:T(8,128)S(1)} %middle.1.inner, bf16[8,272,128]{2,1,0:T(8,128)(2,1)S(1)} %all-to-all-done.flow, f32[24,128]{1,0:T(8,128)S(1)} %get-tuple-element.30.levels, bf16[3,64,128]{2,1,0:T(8,128)(2,1)S(1)} %collective-permute-done.3.after.mate, ...), custom_call_target="tpu_custom_call" | custom-call | tf_op jit(solution)/shard_map/transported/pallas_call | solution.py:606
  (4 shorter events, 0.0 us)
Async XLA Ops:
  2.4 19.1 %all-to-all-start = ((bf16[8,272,128]{2,1,0:T(8,128)(2,1)}), bf16[8,272,128]{2,1,0:T(8,128)(2,1)S(1)}, u32[]{:S(2)}, u32[]{:S(2)}) async-start(bf16[8,272,128]{2,1,0:T(8,128)(2,1)} %get-tuple-element.29), calls=%async_computation | async-start | bytes 1114112 | tf_op jit(solution)/shard_map/all_to_all | solution.py:557
  8.1 2.1 %collective-permute-start = (bf16[3,64,128]{2,1,0:T(8,128)(2,1)S(1)}, bf16[3,64,128]{2,1,0:T(8,128)(2,1)S(1)}, u32[]{:S(2)}, u32[]{:S(2)}) collective-permute-start(bf16[3,64,128]{2,1,0:T(8,128)(2,1)S(1)} %get-tuple-element.26), channel_id=1, source_target_pairs={{0,8},{8,0},{16,24},{24,16},{32,40},{40,32},{48,56},{56,48},{64,72... | collective-permute-start | bytes 147464 | tf_op jit(solution)/shard_map/ppermute | solution.py:556
  10.3 7.3 %copy-start = (s32[32,4]{0,1:T(4,128)S(1)}, s32[32,4]{0,1:T(4,128)}, u32[]{:S(2)}) copy-start(s32[32,4]{0,1:T(4,128)} %param.13) | copy-start | bytes 1540
  10.3 10.0 %collective-permute-start.1 = (bf16[3,64,128]{2,1,0:T(8,128)(2,1)S(1)}, bf16[3,64,128]{2,1,0:T(8,128)(2,1)S(1)}, u32[]{:S(2)}, u32[]{:S(2)}) collective-permute-start(bf16[3,64,128]{2,1,0:T(8,128)(2,1)S(1)} %pad_maximum_fusion), channel_id=1, source_target_pairs={{0,16},{24,40},{32,48},{56,72},{64,80},{88,104},{96,112},{120,136}... | collective-permute-start | bytes 147464 | tf_op jit(solution)/shard_map/ppermute | solution.py:515
  20.3 1.2 %collective-permute-start.2 = (bf16[3,64,128]{2,1,0:T(8,128)(2,1)S(1)}, bf16[3,64,128]{2,1,0:T(8,128)(2,1)S(1)}, u32[]{:S(2)}, u32[]{:S(2)}) collective-permute-start(bf16[3,64,128]{2,1,0:T(8,128)(2,1)S(1)} %collective-permute-done.1.own), channel_id=1, source_target_pairs={{0,8},{8,0},{16,24},{24,16},{32,40},{40,32},{48,56},{56,48},{64,72... | collective-permute-start | bytes 147464 | tf_op jit(solution)/shard_map/ppermute | solution.py:583
  22.4 1.3 %collective-permute-start.3 = (bf16[3,64,128]{2,1,0:T(8,128)(2,1)S(1)}, bf16[3,64,128]{2,1,0:T(8,128)(2,1)S(1)}, u32[]{:S(2)}, u32[]{:S(2)}) collective-permute-start(bf16[3,64,128]{2,1,0:T(8,128)(2,1)S(1)} %get-tuple-element.40), channel_id=1, source_target_pairs={{0,8},{8,0},{16,24},{24,16},{32,40},{40,32},{48,56},{56,48},{64,72... | collective-permute-start | bytes 147464 | tf_op jit(solution)/shard_map/ppermute | solution.py:592
  23.7 8.2 %collective-permute-start.4 = (bf16[3,64,128]{2,1,0:T(8,128)(2,1)S(1)}, bf16[3,64,128]{2,1,0:T(8,128)(2,1)S(1)}, u32[]{:S(2)}, u32[]{:S(2)}) collective-permute-start(bf16[3,64,128]{2,1,0:T(8,128)(2,1)S(1)} %pad_maximum_fusion.1), channel_id=1, source_target_pairs={{0,16},{24,40},{32,48},{56,72},{64,80},{88,104},{96,112},{120,136}... | collective-permute-start | bytes 147464 | tf_op jit(solution)/shard_map/ppermute | solution.py:515
  31.9 1.3 %collective-permute-start.5 = (bf16[3,64,128]{2,1,0:T(8,128)(2,1)S(1)}, bf16[3,64,128]{2,1,0:T(8,128)(2,1)S(1)}, u32[]{:S(2)}, u32[]{:S(2)}) collective-permute-start(bf16[3,64,128]{2,1,0:T(8,128)(2,1)S(1)} %collective-permute-done.4.own), channel_id=1, source_target_pairs={{0,8},{8,0},{16,24},{24,16},{32,40},{40,32},{48,56},{56,48},{64,72... | collective-permute-start | bytes 147464 | tf_op jit(solution)/shard_map/ppermute | solution.py:605
